TPU v7x, 32 devices: a whole 2x2x4 slice. The times are simulated.
32 devices in a mesh: groups: 2 (over y), patch: 4 (over x, core), tensor: 4 (over z).
Axes of the slice: x: 2, y: 2, z: 4, core: 2. Of those that a mesh axis runs over, the one named last changes fastest.
Arguments:
- source: bfloat16 [8192, 69, 128], P(('groups', 'patch', 'tensor')), parts along dimension 0, may hold values from -48 to 48
- intersection_tiles: bfloat16 [4096, 2, 128, 128], P(('patch', 'tensor')), may hold values from 0.0009994507 to 1
- send_index: int32 [16, 16, 2], P(('patch', 'tensor')), may hold values from 0 to 255, as said below
- intersection: int32 [4096, 2], P(('patch', 'tensor')), may hold values from 0 to 31, as said below
- emb_weight: bfloat16 [69, 256, 2048], P(None, 'tensor'), may hold values from -0.046875 to 0.046875
- norm_gain: float32 [2048], replicated, may hold values from 0.1 to 1.9
- attention_in: bfloat16 [2048, 3, 2048], P(None, None, 'tensor'), may hold values from -1 to 1
- attention_out: bfloat16 [2048, 2048], P('tensor'), may hold values from -0.125 to 0.125
Outputs:
- layer_out: bfloat16 [4096, 2048], P(('groups', 'patch', 'tensor')), parts along dimension 0
There are 2 independent parts, one for each index of `groups`. A program takes and returns all parts, laid end to end along the dimension named above; an argument that names none is the same for every part. Nothing has to cross between parts.
Inputs may be any that keep to these rules, and one draw needn't show every extreme that they name: send_index[q, r, s] is a block of sender q's own 256 source blocks. A device names at most 2 slots of one sender in its intersection entries, and exactly 2 of at least one sender; every slot q * 2 + s that a device names is filled by sender q.
All inputs are finite; a program needn't handle non-finite values.
Results may differ from a plain program's by a relative error of at most 0.0085.
Values may be sent and summed in bfloat16 or wider, within the bound.
A program may use at most 192 MiB of HBM per device.

v0:
```python
import jax
import jax.numpy as jnp
from jax import lax
from jax.sharding import PartitionSpec as P

HD = 128


EPS = 1e-05


def on_device(
    source,
    intersection_tiles,
    send_index,
    intersection,
    emb_weight,
    norm_gain,
    attention_in,
    attention_out,
):
    n_tensor = lax.axis_size("tensor")
    blocks_here, channels, cell_rows = source.shape
    targets, depth, tile_rows, pix_block = intersection_tiles.shape
    peers = send_index.shape[1]
    slots = send_index.shape[2]
    payload = jnp.take(source, send_index.reshape(-1), axis=0).reshape(
        peers, slots, channels, cell_rows
    )
    arrived = lax.all_to_all(payload, ("patch", "tensor"), split_axis=0, concat_axis=0, tiled=True)
    arrived = arrived.reshape(peers * slots, channels, cell_rows)
    picked = jnp.take(arrived, intersection.reshape(-1), axis=0)
    tok_local = targets // 2
    half_tensor = n_tensor // 2
    sub_pix = pix_block // half_tensor
    picked = picked.reshape(tok_local, 2, depth, channels, cell_rows)
    tile_view = intersection_tiles.reshape(tok_local, 2, depth, tile_rows, half_tensor, sub_pix)
    numer = jnp.einsum("thkcr,thkrap->hactp", picked, tile_view, preferred_element_type=jnp.float32)
    area = jnp.sum(tile_view, axis=(2, 3), dtype=jnp.float32)
    area = jnp.transpose(area, (1, 2, 0, 3))[:, :, None]
    regridded = (numer / area).astype(jnp.bfloat16).reshape(n_tensor, channels, tok_local * sub_pix)
    arrived_pixels = lax.all_to_all(regridded, "tensor", split_axis=0, concat_axis=2, tiled=True)
    tok_rows = n_tensor * tok_local
    pixels = arrived_pixels.reshape(channels, tok_rows, sub_pix)
    embed_sum = lax.psum(
        jnp.einsum("ctq,cqd->td", pixels, emb_weight, preferred_element_type=jnp.float32), "tensor"
    )
    embedded = embed_sum.astype(jnp.bfloat16)
    values_f = embedded.astype(jnp.float32)
    factor = lax.rsqrt(jnp.mean(values_f * values_f, axis=-1, keepdims=True) + EPS)
    normed = (values_f * factor * norm_gain).astype(jnp.bfloat16)
    own_rows = lax.dynamic_slice_in_dim(
        embedded, lax.axis_index("tensor") * tok_local, tok_local, 0
    )
    width = normed.shape[1]
    heads_here = attention_in.shape[2] // HD
    projected = jnp.dot(normed, attention_in.reshape(width, -1), preferred_element_type=jnp.float32)
    projected = projected.reshape(tok_rows, 3, heads_here, HD)
    query = (projected[:, 0] * HD ** (-0.5)).astype(jnp.bfloat16)
    keys_local = projected[:, 1].astype(jnp.bfloat16)
    values_local = projected[:, 2].astype(jnp.bfloat16)
    running_max = jnp.full((heads_here, tok_rows), -1e30, jnp.float32)
    key_piece = lax.all_gather(keys_local, "patch", axis=0, tiled=True)
    value_piece = lax.all_gather(values_local, "patch", axis=0, tiled=True)
    scores = jnp.einsum("qhd,khd->hqk", query, key_piece, preferred_element_type=jnp.float32)
    new_max = jnp.maximum(running_max, jnp.max(scores, axis=-1))
    expo = jnp.exp(scores - new_max[..., None])
    new_sum = jnp.sum(expo, axis=-1)
    update = jnp.einsum(
        "hqk,khd->hqd", expo.astype(jnp.bfloat16), value_piece, preferred_element_type=jnp.float32
    )
    heads_out = (update / new_sum[..., None]).astype(jnp.bfloat16)
    heads_out = jnp.transpose(heads_out, (1, 0, 2)).reshape(tok_rows, heads_here * HD)
    mixing = lax.psum_scatter(
        jnp.dot(heads_out, attention_out, preferred_element_type=jnp.float32).astype(jnp.bfloat16),
        "tensor",
        scatter_dimension=0,
        tiled=True,
    ).astype(jnp.float32)
    return (own_rows.astype(jnp.float32) + mixing).astype(jnp.bfloat16)


def solution(mesh):
    placed = (
        P(("groups", "patch", "tensor"), None, None),
        P(("patch", "tensor"), None, None, None),
        P(("patch", "tensor"), None, None),
        P(("patch", "tensor"), None),
        P(None, "tensor", None),
        P(),
        P(None, None, "tensor"),
        P("tensor", None),
    )
    return jax.shard_map(
        on_device,
        mesh=mesh,
        in_specs=placed,
        out_specs=P(("groups", "patch", "tensor"), None),
        check_vma=False,
    )
```

profile of v0, /device:TPU:0, one launch (start us, length us, event | category | flops | bytes accessed | tf_op | source)
XLA Modules:
  0.0 548.7 jit_solution(12589537057766214320)
XLA Ops:
  6.5 0.9 copy.33
  8.3 3.3 gather_fusion
  11.7 1.4 broadcast_select_fusion.1
  13.0 7.4 %all-to-all-start = ((bf16[16,2,69,128]{3,1,2,0:T(2,128)(2,1)}), bf16[16,2,69,128]{3,1,2,0:T(2,128)(2,1)S(1)}, u32[]{:S(2)}, u32[]{:S(2)}) async-start(bf16[16,2,69,128]{3,1,2,0:T(2,128)(2,1)} %broadcast_select_fusion.1), calls=%async_computation | async-start | bytes 1130496 | tf_op jit(solution)/shard_map/all_to_all | solution.py:30
  22.2 0.9 copy.31
  23.1 22.4 %copy.38 = bf16[256,2,128,128]{2,3,1,0:T(8,128)(2,1)} copy(bf16[256,2,128,128]{3,2,1,0:T(8,128)(2,1)} %param.9) | data formatting | bytes 33554432 | tf_op args[1]
  45.5 6.9 %convert_reduce_fusion = f32[256,128]{1,0:T(8,128)S(1)} fusion(bf16[256,2,128,128]{3,2,1,0:T(8,128)(2,1)} %param.9), kind=kLoop, calls=%fused_computation.2 | loop fusion | flops 16744448 | bytes 16908288 | tf_op jit(solution)/shard_map/reduce_sum | solution.py:39
  52.4 0.9 reduce_sum.30
  53.4 14.6 %gather_fusion.1 = bf16[512,69,128]{2,1,0:T(8,128)(2,1)} fusion(bf16[32,69,128]{2,1,0:T(8,128)(2,1)S(1)} %bitcast.72, s32[1024]{0:T(1024)S(1)} %pad_clamp_fusion), kind=kCustom, calls=%fused_computation.1 | custom fusion | bytes 18089984 | tf_op jit(solution)/shard_map/jit(_take)/gather | solution.py:32
  68.0 9.4 %copy.37 = bf16[512,69,128]{2,0,1:T(8,128)(2,1)} copy(bf16[512,69,128]{2,1,0:T(8,128)(2,1)} %gather_fusion.1) | data formatting | bytes 18087936 | tf_op jit(solution)/shard_map/jit(_take)/gather | solution.py:32
  77.4 12.1 %fusion.6 = bf16[128,2,2,69,128,1]{4,2,1,0,3,5:T(2,128)(2,1)} fusion(bf16[128,2,2,69,128]{4,2,1,0,3:T(2,128)(2,1)} %bitcast.73, pred[128,2,2]{2,1,0:T(4,128)(4,1)S(1)} %copy.31), kind=kLoop, calls=%fused_computation.12 | loop fusion | flops 4521984 | bytes 18088448 | tf_op jit(solution)/shard_map/jit(_take)/select_n | solution.py:32
  89.5 14.1 %fusion = bf16[2,2,69,128,64]{2,4,1,3,0:T(8,128)(2,1)} fusion(bf16[128,2,2,128,2,64]{3,5,4,2,1,0:T(8,128)(2,1)} %bitcast.74, bf16[128,2,2,69,128,1]{4,2,1,0,3,5:T(2,128)(2,1)} %fusion.6, f32[128,2,2,64]{3,2,1,0:T(2,128)S(1)} %copy-done.1), kind=kOutput, calls=%fused_computation.5 | convolution fusion | flops 1162149888 | bytes 30474240 | tf_op jit(solution)/shard_map/thkcr,thkrap->hactp/dot_general | solution.py:38
  103.7 18.8 %copy.42 = bf16[2,2,69,128,64]{4,3,2,1,0:T(8,128)(2,1)} copy(bf16[2,2,69,128,64]{2,4,1,3,0:T(8,128)(2,1)} %fusion) | data formatting | bytes 9043968 | tf_op jit(solution)/shard_map/convert_element_type | solution.py:41
  122.5 10.6 %reshape.133 = bf16[4,69,8192]{2,1,0:T(8,128)(2,1)} reshape(bf16[2,2,69,128,64]{4,3,2,1,0:T(8,128)(2,1)} %copy.42) | data formatting | bytes 9043968 | tf_op jit(solution)/shard_map/reshape | solution.py:41
  133.1 5.0 all-to-all-start.1
  138.1 8.9 %copy.45 = bf16[2048,3,512]{0,2,1:T(8,128)(2,1)} copy(bf16[2048,3,512]{2,0,1:T(8,128)(2,1)} %param.14) | data formatting | bytes 12582912 | tf_op args[6]
  146.9 96.4 %all-to-all-done.1 = bf16[4,69,8192]{2,1,0:T(8,128)(2,1)} async-done(((bf16[4,69,8192]{2,1,0:T(8,128)(2,1)}), bf16[4,69,8192]{2,1,0:T(8,128)(2,1)}, u32[]{:S(2)}, u32[]{:S(2)}) %all-to-all-start.1) | async-done | bytes 4522016 | tf_op jit(solution)/shard_map/all_to_all | solution.py:42
  243.3 7.9 %copy.43 = bf16[1,69,4,8192]{3,2,1,0:T(4,128)(2,1)} copy(bf16[1,69,4,8192]{3,1,2,0:T(8,128)(2,1)} %bitcast.14) | data formatting | bytes 9043968 | tf_op jit(solution)/shard_map/all_to_all | solution.py:42
  251.2 14.1 %reshape.134 = bf16[69,512,64]{2,1,0:T(8,128)(2,1)} reshape(bf16[1,69,4,8192]{3,2,1,0:T(4,128)(2,1)} %copy.43) | data formatting | bytes 9043968 | tf_op jit(solution)/shard_map/reshape | solution.py:44
  265.4 16.2 %convolution_bitcast_fusion = f32[512,2048]{1,0:T(8,128)} fusion(bf16[69,512,64]{2,1,0:T(8,128)(2,1)} %reshape.134, bf16[69,64,2048]{2,1,0:T(8,128)(2,1)} %param.12), kind=kOutput, calls=%fused_computation.20 | convolution fusion | flops 9261023232 | bytes 26804224 | tf_op jit(solution)/shard_map/ctq,cqd->td/dot_general | solution.py:46
  281.6 145.6 %all-reduce.1 = bf16[512,2048]{1,0:T(8,128)(2,1)} all-reduce(f32[512,2048]{1,0:T(8,128)} %convolution_bitcast_fusion), channel_id=1, replica_groups=mesh['groups'=2,'patch'=4,'tensor'=4] {'tensor'}, use_global_device_ids=true, to_apply=%region_1.2 | all-reduce | flops 1048576 | bytes 6291456 | tf_op jit(solution)/shard_map/psum | solution.py:45
  427.2 2.1 fusion.10
  429.3 7.5 %fusion.41 = (bf16[512,3,4,128]{3,0,2,1:T(8,128)(2,1)S(1)}, f32[512,3,4,128]{3,0,2,1:T(8,128)}) fusion(bf16[3,4,128,2048]{3,2,1,0:T(8,128)(2,1)} %bitcast.75, bf16[512,2048]{1,0:T(8,128)(2,1)} %all-reduce.1, f32[2048]{0:T(1024)S(1)} %copy-done.2, f32[512]{0:T(512)S(1)} %add_rsqrt_fusion), kind=kOutput, calls=%fused_computation.50 | convolution fusion | flops 3226206208 | bytes 13117440 | tf_op jit(solution)/shard_map/dot_general | solution.py:57
  436.7 1.0 fusion.40
  438.6 21.2 %all-gather.5.cloned.1.call-done = bf16[2048,1,4,128]{3,0,2,1:T(8,128)(2,1)} async-done(((bf16[512,1,4,128]{3,0,2,1:T(8,128)(2,1)}), bf16[2048,1,4,128]{3,0,2,1:T(8,128)(2,1)}) %all-gather.5.cloned.1.call-update) | async-done | bytes 2097168 | tf_op jit(solution)/shard_map/all_gather | solution.py:63
  459.8 10.5 %fusion.42 = (f32[4,512]{1,0:T(4,128)S(1)}, f32[4,512,2048]{2,1,0:T(8,128)}) fusion(bf16[2048,1,4,128]{3,0,2,1:T(8,128)(2,1)} %all-gather.5.cloned.1.call-done, f32[512,3,4,128]{3,0,2,1:T(8,128)} %get-tuple-element.8), kind=kOutput, calls=%fused_computation.51 | convolution fusion | flops 1078458368 | bytes 19931136 | tf_op jit(solution)/shard_map/qhd,khd->hqk/dot_general | solution.py:65
  470.3 8.2 %fusion.3 = f32[4,512]{1,0:T(4,128)S(1)} fusion(f32[4,512,2048]{2,1,0:T(8,128)} %get-tuple-element.10, f32[4,512]{1,0:T(4,128)S(1)} %broadcast_maximum_fusion), kind=kLoop, calls=%fused_computation.9 | loop fusion | flops 8386560 | bytes 16793600 | tf_op jit(solution)/shard_map/reduce_sum | solution.py:68
  478.5 5.5 %all-gather.7.cloned.1.call-done = bf16[2048,1,4,128]{3,0,2,1:T(8,128)(2,1)} async-done(((bf16[512,1,4,128]{3,0,2,1:T(8,128)(2,1)}), bf16[2048,1,4,128]{3,0,2,1:T(8,128)(2,1)}) %all-gather.7.cloned.1.call-update) | async-done | bytes 2097168 | tf_op jit(solution)/shard_map/all_gather | solution.py:64
  484.0 9.4 %divide_convert_fusion = bf16[512,4,128]{0,2,1:T(8,128)(2,1)S(1)} fusion(bf16[2048,1,4,128]{3,0,2,1:T(8,128)(2,1)} %all-gather.7.cloned.1.call-done, f32[4,512,2048]{2,1,0:T(8,128)} %get-tuple-element.10, f32[4,512]{1,0:T(4,128)S(1)} %broadcast_maximum_fusion, f32[512,4]{0,1:T(4,128)S(1)} %bitcast.78), kind=kOutput, calls=%fused_computation.34 | convolution fusion | flops 1082654720 | bytes 19415040 | tf_op jit(solution)/shard_map/hqk,khd->hqd/dot_general | solution.py:69
  493.4 2.6 convolution_convert_fusion
  496.0 44.0 %reduce-scatter.2.cloned.1.call-done = bf16[128,2048]{1,0:T(8,128)(2,1)} async-done(((bf16[512,2048]{1,0:T(8,128)(2,1)}), bf16[128,2048]{1,0:T(8,128)(2,1)}) %reduce-scatter.2.cloned.1.call-update) | async-done | bytes 524304 | tf_op jit(solution)/shard_map/reduce_scatter | solution.py:74
  540.0 2.1 add_convert_fusion
  (27 shorter events, 3.6 us)
Async XLA Ops:
  6.5 486.8 %copy-start = (bf16[512,2048]{1,0:T(8,128)(2,1)S(1)}, bf16[512,2048]{1,0:T(8,128)(2,1)}, u32[]{:S(2)}) copy-start(bf16[512,2048]{1,0:T(8,128)(2,1)} %param.15) | copy-start | bytes 6291460
  13.0 40.3 %all-to-all-start = ((bf16[16,2,69,128]{3,1,2,0:T(2,128)(2,1)}), bf16[16,2,69,128]{3,1,2,0:T(2,128)(2,1)S(1)}, u32[]{:S(2)}, u32[]{:S(2)}) async-start(bf16[16,2,69,128]{3,1,2,0:T(2,128)(2,1)} %broadcast_select_fusion.1), calls=%async_computation | async-start | bytes 1130496 | tf_op jit(solution)/shard_map/all_to_all | solution.py:30
  77.4 12.1 %copy-start.1 = (f32[128,2,2,64]{3,2,1,0:T(2,128)S(1)}, f32[128,2,2,64]{3,2,1,0:T(2,128)}, u32[]{:S(2)}) copy-start(f32[128,2,2,64]{3,2,1,0:T(2,128)} %reduce_sum.30) | copy-start | bytes 393220
  133.1 110.2 %all-to-all-start.1 = ((bf16[4,69,8192]{2,1,0:T(8,128)(2,1)}), bf16[4,69,8192]{2,1,0:T(8,128)(2,1)}, u32[]{:S(2)}, u32[]{:S(2)}) async-start(bf16[4,69,8192]{2,1,0:T(8,128)(2,1)} %reshape.133), calls=%async_computation.1 | async-start | bytes 9437184 | tf_op jit(solution)/shard_map/all_to_all | solution.py:42
  138.1 321.8 %all-gather.5.cloned.1.call-start = ((), (), s32[]{:S(2)}) async-start(), calls=%async_computation.4 | async-start | bytes 2621440 | tf_op jit(solution)/shard_map/all_gather | solution.py:63
  281.5 147.7 %copy-start.2 = (f32[2048]{0:T(1024)S(1)}, f32[2048]{0:T(1024)}, u32[]{:S(2)}) copy-start(f32[2048]{0:T(1024)} %param.13) | copy-start | bytes 24580
  437.8 46.2 %all-gather.7.cloned.1.call-start = ((), (), s32[]{:S(2)}) async-start(), calls=%async_computation.5 | async-start | bytes 2621440 | tf_op jit(solution)/shard_map/all_gather | solution.py:64
  438.6 101.5 %reduce-scatter.2.cloned.1.call-start = ((), (), s32[]{:S(2)}) async-start(), calls=%async_computation.3 | async-start | bytes 2621440 | tf_op jit(solution)/shard_map/reduce_scatter | solution.py:74
Sparse Core Ops, SparseCore 0:
  437.9 21.8 all-gather.4
  461.4 22.5 all-gather.6
  496.1 43.8 reduce-scatter.1
where the time goes:
time: 551 us; the launch traced here: 549 us
  waiting for transfers between devices  168 us (30%)
  blocking collectives  146 us (26%)
  local copies, waits for them, and re-layouts  116 us (21%)
  matrix products  60.3 us (11%)
  other arithmetic  33.5 us (6%)
  between operations  13.2 us (2%)
  starting transfers between devices  12.4 us (2%)
    psum x1, blocking collectives, on_device(): lax.psum(jnp.einsum('ctq,cqd->td', pixels, emb_weight, preferred_element_...  146 us
    all_to_all x1, waiting for transfers between devices, on_device(): lax.all_to_all(regridded, 'tensor', split_axis=0, concat_axis=2, tiled=True)  96.4 us
    reduce_scatter x1, waiting for transfers between devices, on_device(): lax.psum_scatter(jnp.dot(heads_out, attention_out, preferred_element_type...  44 us
    unnamed x10, local copies, waits for them, and re-layouts  33 us
    gather x2, local copies, waits for them, and re-layouts, on_device(): picked = jnp.take(arrived, intersection.reshape(-1), axis=0)  24 us
    all_gather x1, waiting for transfers between devices, on_device(): key_piece = lax.all_gather(keys_local, 'patch', axis=0, tiled=True)  21.2 us
    convert_element_type x1, local copies, waits for them, and re-layouts, on_device(): (numer / area).astype(jnp.bfloat16)  18.8 us
    dot_general x1, matrix products, on_device(): jnp.einsum('ctq,cqd->td', pixels, emb_weight, preferred_element_type=jnp....  16.2 us
  transfers between devices with their start and end apart: 5, of which 4 were waited for; matrix products, arithmetic and copies ran while one was open for 11% of the time, Pallas kernels for 0%

commit v1 on v0

v1 whole, which is shorter than its diff:
```python
import functools

import jax
import jax.numpy as jnp
from jax import lax
from jax.experimental import pallas as pl
from jax.experimental.pallas import tpu as pltpu
from jax.sharding import PartitionSpec as P

HD = 128
EPS = 1e-05
LANES = 128
MIB = 1 << 20


def round_up(value, unit):
    return -(-value // unit) * unit


def regrid_kernel(channels, toks, slot_ref, arrived_ref, tiles_ref, out_ref, ordered, stage):
    pairs = (channels + 1) // 2
    half = round_up(pairs + 1, 8)
    step = pl.program_id(0)

    @pl.when(step == 0)
    def _():
        row = lax.broadcasted_iota(jnp.int32, (2 * half, channels), 0)
        col = lax.broadcasted_iota(jnp.int32, (2 * half, channels), 1)
        wanted = jnp.where(row < half, 2 * row, 2 * (row - half) + 1)
        order = jnp.where(wanted == col, 1.0, 0.0).astype(jnp.bfloat16)
        ones = lax.broadcasted_iota(jnp.int32, (2 * half, LANES), 0) == pairs

        @pl.loop(0, arrived_ref.shape[0])
        def _(slot):
            moved = jnp.dot(order, arrived_ref[slot], preferred_element_type=jnp.float32)
            keep = lax.broadcasted_iota(jnp.int32, (2 * half, LANES), 0)
            valid = ((keep < pairs) | ((keep >= half) & (keep < half + channels // 2)))
            moved = jnp.where(valid, moved, 0.0)
            ordered[slot] = jnp.where(ones, 1.0, moved).astype(jnp.bfloat16)

    low = lax.broadcasted_iota(jnp.int32, (half, LANES), 1) < LANES // 2
    for tok in range(toks):
        for side in range(2):
            block = tok * 2 + side
            base = (step * toks * 2 + block) * 2
            lhs = jnp.concatenate([ordered[slot_ref[base]], ordered[slot_ref[base + 1]]], axis=1)
            rhs = tiles_ref[block].reshape(2 * tiles_ref.shape[2], LANES)
            numer = jnp.dot(lhs, rhs, preferred_element_type=jnp.float32)
            area = numer[pairs : pairs + 1]
            value = numer / area
            even, odd = value[:half], value[half:]
            first = jnp.where(low, even, pltpu.roll(odd, LANES // 2, 1))
            second = jnp.where(low, pltpu.roll(even, LANES // 2, 1), odd)
            start = 2 * side * pairs * toks + tok
            stage[pl.ds(start, pairs, stride=toks), :] = first[:pairs]
            stage[pl.ds(start + pairs * toks, pairs, stride=toks), :] = second[:pairs]
    out_ref[...] = stage[...].reshape(4, pairs, toks, LANES).astype(jnp.bfloat16)


def regrid(arrived, tiles, slots, toks=16):
    n_slots, channels, cells = arrived.shape
    blocks = tiles.shape[0]
    tok_local = blocks // 2
    pairs = (channels + 1) // 2
    half = round_up(pairs + 1, 8)
    return pl.pallas_call(
        functools.partial(regrid_kernel, channels, toks),
        out_shape=jax.ShapeDtypeStruct((4, pairs, tok_local, LANES), jnp.bfloat16),
        grid_spec=pltpu.PrefetchScalarGridSpec(
            num_scalar_prefetch=1,
            grid=(tok_local // toks,),
            in_specs=[
                pl.BlockSpec((n_slots, channels, cells), lambda i, s: (0, 0, 0)),
                pl.BlockSpec((2 * toks,) + tiles.shape[1:], lambda i, s: (i, 0, 0, 0)),
            ],
            out_specs=pl.BlockSpec((4, pairs, toks, LANES), lambda i, s: (0, 0, i, 0)),
            scratch_shapes=[
                pltpu.VMEM((n_slots, 2 * half, cells), jnp.bfloat16),
                pltpu.VMEM((4 * pairs * toks, LANES), jnp.float32),
            ],
        ),
        compiler_params=pltpu.CompilerParams(vmem_limit_bytes=40 * MIB),
        name="regrid",
    )(slots, arrived, tiles)


def embed_kernel(pairs, per, channels, px_ref, w_ref, out_ref, lhs, acc):
    step = pl.program_id(0)
    last = pl.num_programs(0) - 1
    senders, _, toks, _ = px_ref.shape
    width = out_ref.shape[1]
    tile = 512

    @pl.when(step == 0)
    def _():
        acc[...] = jnp.zeros_like(acc)

    def multiply(count, rows):
        for s in range(senders):
            for j in range(count):
                lhs[s * toks : (s + 1) * toks, j * LANES : (j + 1) * LANES] = px_ref[s, j]

        @pl.loop(0, width // tile)
        def _(i):
            cols = pl.ds(pl.multiple_of(i * tile, tile), tile)
            w = w_ref[: 2 * count, :, cols].reshape(count * LANES, tile)
            if rows < count * LANES:
                place = lax.broadcasted_iota(jnp.int32, w.shape, 0)
                w = jnp.where(place < rows, w, jnp.zeros_like(w))
            acc[:, cols] += jnp.dot(
                lhs[:, : count * LANES], w, preferred_element_type=jnp.float32
            )

    @pl.when(step < last)
    def _():
        multiply(per, per * LANES)

    @pl.when(step == last)
    def _():
        before = (pairs - 1) // per * per
        multiply(pairs - before, (channels - 2 * before) * (LANES // 2))
        out_ref[...] = acc[...].astype(out_ref.dtype)


def embed(pixels, weight, per=6):
    senders, pairs, toks, _ = pixels.shape
    channels, sub_pix, width = weight.shape
    return pl.pallas_call(
        functools.partial(embed_kernel, pairs, per, channels),
        out_shape=jax.ShapeDtypeStruct((senders * toks, width), jnp.bfloat16),
        grid=(pl.cdiv(pairs, per),),
        in_specs=[
            pl.BlockSpec((senders, per, toks, LANES), lambda i: (0, i, 0, 0)),
            pl.BlockSpec((2 * per, sub_pix, width), lambda i: (i, 0, 0)),
        ],
        out_specs=pl.BlockSpec((senders * toks, width), lambda i: (0, 0)),
        scratch_shapes=[
            pltpu.VMEM((senders * toks, per * LANES), jnp.bfloat16),
            pltpu.VMEM((senders * toks, width), jnp.float32),
        ],
        compiler_params=pltpu.CompilerParams(vmem_limit_bytes=48 * MIB),
        name="embed",
    )(pixels, weight)


def attend_kernel(q_ref, k_ref, v_ref, out_ref):
    scores = lax.dot_general(
        q_ref[...], k_ref[...], (((1,), (1,)), ((), ())), preferred_element_type=jnp.float32
    )
    highest = jnp.max(scores, axis=-1, keepdims=True)
    expo = jnp.exp(scores - highest)
    denom = jnp.sum(expo, axis=-1, keepdims=True)
    summed = jnp.dot(expo.astype(jnp.bfloat16), v_ref[...], preferred_element_type=jnp.float32)
    out_ref[...] = (summed / denom).astype(jnp.bfloat16)


def attend(query, keys, values, rows=256):
    tokens, width = query.shape
    all_tokens = keys.shape[0]
    return pl.pallas_call(
        attend_kernel,
        out_shape=jax.ShapeDtypeStruct(query.shape, jnp.bfloat16),
        grid=(width // HD, tokens // rows),
        in_specs=[
            pl.BlockSpec((rows, HD), lambda h, i: (i, h)),
            pl.BlockSpec((all_tokens, HD), lambda h, i: (0, h)),
            pl.BlockSpec((all_tokens, HD), lambda h, i: (0, h)),
        ],
        out_specs=pl.BlockSpec((rows, HD), lambda h, i: (i, h)),
        compiler_params=pltpu.CompilerParams(vmem_limit_bytes=48 * MIB),
        name="attend",
    )(query, keys, values)


def general_embed(arrived, intersection_tiles, intersection, emb_weight, n_tensor):
    targets, depth, tile_rows, pix_block = intersection_tiles.shape
    _, channels, cell_rows = arrived.shape
    picked = jnp.take(arrived, intersection.reshape(-1), axis=0)
    tok_local = targets // 2
    half_tensor = n_tensor // 2
    sub_pix = pix_block // half_tensor
    picked = picked.reshape(tok_local, 2, depth, channels, cell_rows)
    tile_view = intersection_tiles.reshape(tok_local, 2, depth, tile_rows, half_tensor, sub_pix)
    numer = jnp.einsum("thkcr,thkrap->hactp", picked, tile_view, preferred_element_type=jnp.float32)
    area = jnp.sum(tile_view, axis=(2, 3), dtype=jnp.float32)
    area = jnp.transpose(area, (1, 2, 0, 3))[:, :, None]
    regridded = (numer / area).astype(jnp.bfloat16).reshape(n_tensor, channels, tok_local * sub_pix)
    moved = lax.all_to_all(regridded, "tensor", split_axis=0, concat_axis=2, tiled=True)
    pixels = moved.reshape(channels, n_tensor * tok_local, sub_pix)
    return jnp.einsum(
        "ctq,cqd->td", pixels, emb_weight, preferred_element_type=jnp.float32
    ).astype(jnp.bfloat16)


def on_device(
    source,
    intersection_tiles,
    send_index,
    intersection,
    emb_weight,
    norm_gain,
    attention_in,
    attention_out,
):
    n_tensor = lax.axis_size("tensor")
    blocks_here, channels, cell_rows = source.shape
    peers = send_index.shape[1]
    slots = send_index.shape[2]
    payload = jnp.take(source, send_index.reshape(-1), axis=0, mode="clip").reshape(
        peers, slots, channels, cell_rows
    )
    arrived = lax.all_to_all(payload, ("patch", "tensor"), split_axis=0, concat_axis=0, tiled=True)
    arrived = arrived.reshape(peers * slots, channels, cell_rows)
    if 2 * emb_weight.shape[1] == LANES and intersection_tiles.shape[0] % 32 == 0:
        pixels = regrid(arrived, intersection_tiles, intersection.reshape(-1))
        pixels = lax.all_to_all(pixels, "tensor", split_axis=0, concat_axis=0, tiled=True)
        partial = embed(pixels, emb_weight)
    else:
        partial = general_embed(arrived, intersection_tiles, intersection, emb_weight, n_tensor)
    own_rows = lax.psum_scatter(partial, "tensor", scatter_dimension=0, tiled=True)
    values_f = own_rows.astype(jnp.float32)
    factor = lax.rsqrt(jnp.mean(values_f * values_f, axis=-1, keepdims=True) + EPS)
    normed = (values_f * factor * norm_gain).astype(jnp.bfloat16)
    normed = lax.all_gather(normed, "tensor", axis=0, tiled=True)

    def project(part):
        return jnp.dot(normed, attention_in[:, part], preferred_element_type=jnp.float32)

    keys = lax.all_gather(project(1).astype(jnp.bfloat16), "patch", axis=0, tiled=True)
    values = lax.all_gather(project(2).astype(jnp.bfloat16), "patch", axis=0, tiled=True)
    query = (project(0) * HD ** (-0.5)).astype(jnp.bfloat16)
    heads_out = attend(query, keys, values)
    mixing = lax.psum_scatter(
        jnp.dot(heads_out, attention_out, preferred_element_type=jnp.float32).astype(jnp.bfloat16),
        "tensor",
        scatter_dimension=0,
        tiled=True,
    ).astype(jnp.float32)
    return (values_f + mixing).astype(jnp.bfloat16)


def solution(mesh):
    placed = (
        P(("groups", "patch", "tensor"), None, None),
        P(("patch", "tensor"), None, None, None),
        P(("patch", "tensor"), None, None),
        P(("patch", "tensor"), None),
        P(None, "tensor", None),
        P(),
        P(None, None, "tensor"),
        P("tensor", None),
    )
    return jax.shard_map(
        on_device,
        mesh=mesh,
        in_specs=placed,
        out_specs=P(("groups", "patch", "tensor"), None),
        check_vma=False,
    )
```

time: 551 us -> 387 us (0.70)
  local copies, waits for them, and re-layouts: 116 us -> 10.4 us
  matrix products: 60.3 us -> 14.8 us
  Pallas kernels: 0 us -> 44.3 us
  blocking collectives: 146 us -> 105 us
  other arithmetic: 33.5 us -> 5.23 us
  waiting for transfers between devices: 168 us -> 186 us
    psum x1 -> x0, blocking collectives: 146 us -> none  [on_device(): lax.psum(jnp.einsum('ctq,cqd->td', pixels, emb_weight, preferred_element_...]
    all_to_all x0 -> x1, blocking collectives: none -> 105 us  [on_device(): lax.all_to_all(pixels, 'tensor', split_axis=0, concat_axis=0, tiled=True)]
    all_to_all x1 -> x0, waiting for transfers between devices: 96.4 us -> none  [on_device(): lax.all_to_all(regridded, 'tensor', split_axis=0, concat_axis=2, tiled=True)]
    all_gather x2 -> x3, waiting for transfers between devices: 26.7 us -> 82.8 us  [the longest x1 45.4 us: on_device(): normed = lax.all_gather(normed, 'tensor', axis=0, tiled=True)]
    dot_general x5 -> x3, matrix products: 57.7 us -> 12.3 us  [project(): jnp.dot(normed, attention_in[:, part], preferred_element_type=jnp.float32)]
    pallas_call x0 -> x3, Pallas kernels: none -> 44.3 us  [the longest x1 17.6 us: embed(): pl.pallas_call(functools.partial(embed_kernel, pairs, per, channels), out...]
    reduce_scatter x0 -> x1, waiting for transfers between devices: none -> 42.8 us  [on_device(): lax.psum_scatter(partial, 'tensor', scatter_dimension=0, tiled=True)]
    unnamed x10 -> x16, local copies, waits for them, and re-layouts: 33 us -> 5.56 us
  transfers between devices with their start and end apart: 5 -> 6, of which waited for: 4 -> 6; matrix products, arithmetic and copies ran while one was open for 11% -> 2% of each run, Pallas kernels for 0% -> 0%
where the time goes in v1:
time: 387 us
  waiting for transfers between devices  186 us (48%)
  blocking collectives  105 us (27%)
  Pallas kernels  44.3 us (11%)
  matrix products  14.8 us (4%)
  between operations  13.3 us (3%)
  local copies, waits for them, and re-layouts  10.4 us (3%)
  starting transfers between devices  7.57 us (2%)
  other arithmetic  5.23 us (1%)
    all_to_all x1, blocking collectives, on_device(): lax.all_to_all(pixels, 'tensor', split_axis=0, concat_axis=0, tiled=True)  105 us
    all_gather x1, waiting for transfers between devices, on_device(): normed = lax.all_gather(normed, 'tensor', axis=0, tiled=True)  45.4 us
    reduce_scatter x1, waiting for transfers between devices, on_device(): lax.psum_scatter(jnp.dot(heads_out, attention_out, preferred_element_type...  44 us
    reduce_scatter x1, waiting for transfers between devices, on_device(): lax.psum_scatter(partial, 'tensor', scatter_dimension=0, tiled=True)  42.8 us
    all_gather x1, waiting for transfers between devices, on_device(): lax.all_gather(project(1).astype(jnp.bfloat16), 'patch', axis=0, tiled=True)  24.1 us
    pallas_call x1, Pallas kernels, embed(): pl.pallas_call(functools.partial(embed_kernel, pairs, per, channels), out...  17.6 us
    pallas_call x1, Pallas kernels, regrid(): pl.pallas_call(functools.partial(regrid_kernel, channels, toks), out_shap...  17.2 us
    all_to_all x1, waiting for transfers between devices, on_device(): lax.all_to_all(payload, ('patch', 'tensor'), split_axis=0, concat_axis=0,...  16.2 us
  transfers between devices with their start and end apart: 6, of which 6 were waited for; matrix products, arithmetic and copies ran while one was open for 2% of the time, Pallas kernels for 0%

profile of v1, /device:TPU:0, one launch (start us, length us, event | category | flops | bytes accessed | tf_op | source)
XLA Modules:
  0.0 386.6 jit_solution(5641651845611581762)
XLA Ops:
  6.5 0.9 copy.15
  7.4 0.1 reshape.25
  7.5 3.3 gather_fusion
  10.9 1.2 copy.16
  12.1 7.4 %all-to-all-start = ((bf16[16,2,69,128]{3,1,2,0:T(2,128)(2,1)}), bf16[16,2,69,128]{3,1,2,0:T(2,128)(2,1)S(1)}, u32[]{:S(2)}, u32[]{:S(2)}) async-start(bf16[16,2,69,128]{3,1,2,0:T(2,128)(2,1)} %copy.16), calls=%async_computation | async-start | bytes 1130496 | tf_op jit(solution)/shard_map/all_to_all | solution.py:212
  19.4 0.0 reduce-scatter.3.cloned.1.call-start
  19.5 0.1 copy.14
  19.6 0.1 reshape.20.slot_ref
  19.8 16.2 %all-to-all-done = bf16[16,2,69,128]{3,1,2,0:T(2,128)(2,1)S(1)} async-done(((bf16[16,2,69,128]{3,1,2,0:T(2,128)(2,1)}), bf16[16,2,69,128]{3,1,2,0:T(2,128)(2,1)S(1)}, u32[]{:S(2)}, u32[]{:S(2)}) %all-to-all-start) | async-done | bytes 565280 | tf_op jit(solution)/shard_map/all_to_all | solution.py:212
  36.0 0.1 copy.17
  36.1 17.2 %regrid.1 = bf16[4,35,128,128]{3,2,1,0:T(8,128)(2,1)S(1)} custom-call(s32[512]{0:T(512)S(1)} %reshape.20.slot_ref, bf16[32,69,128]{2,1,0:T(8,128)(2,1)S(1)} %bitcast.24, bf16[256,2,128,128]{3,2,1,0:T(8,128)(2,1)} %tiles_ref.1), custom_call_target="tpu_custom_call" | custom-call | tf_op jit(solution)/shard_map/regrid/pallas_call | solution.py:66
  53.3 105.2 %all_to_all.10.px_ref = bf16[4,35,128,128]{3,2,1,0:T(8,128)(2,1)} all-to-all(bf16[4,35,128,128]{3,2,1,0:T(8,128)(2,1)S(1)} %regrid.1), channel_id=1, replica_groups=mesh['groups'=2,'patch'=4,'tensor'=4] {'tensor'}, dimensions={0} | all-to-all | bytes 9175040 | tf_op jit(solution)/shard_map/all_to_all | solution.py:216
  158.5 17.6 %embed.1 = bf16[512,2048]{1,0:T(8,128)(2,1)S(1)} custom-call(bf16[4,35,128,128]{3,2,1,0:T(8,128)(2,1)} %all_to_all.10.px_ref, bf16[69,64,2048]{2,1,0:T(8,128)(2,1)} %w_ref.1), custom_call_target="tpu_custom_call" | custom-call | tf_op jit(solution)/shard_map/embed/pallas_call | solution.py:128
  176.0 1.3 copy-done.1
  177.4 0.0 all-gather.4.cloned.1.call-start
  177.4 42.8 %reduce-scatter.3.cloned.1.call-done = bf16[128,2048]{1,0:T(8,128)(2,1)} async-done(((bf16[512,2048]{1,0:T(8,128)(2,1)}), bf16[128,2048]{1,0:T(8,128)(2,1)}) %reduce-scatter.3.cloned.1.call-update) | async-done | bytes 524304 | tf_op jit(solution)/shard_map/reduce_scatter | solution.py:220
  220.2 1.2 fusion.21
  221.5 2.0 fusion.23
  223.5 0.0 all-gather.8.cloned.1.call-start
  223.6 45.4 %all-gather.4.cloned.1.call-done = bf16[512,2048]{1,0:T(8,128)(2,1)} async-done(((bf16[128,2048]{1,0:T(8,128)(2,1)}), bf16[512,2048]{1,0:T(8,128)(2,1)}) %all-gather.4.cloned.1.call-update) | async-done | bytes 2097168 | tf_op jit(solution)/shard_map/all_gather | solution.py:224
  268.9 4.3 %fusion.15 = bf16[512,512]{1,0:T(8,128)(2,1)} fusion(bf16[512,2048]{1,0:T(8,128)(2,1)} %all-gather.4.cloned.1.call-done, bf16[2048,3,512]{2,0,1:T(8,128)(2,1)} %param.14), kind=kOutput, calls=%fused_computation.16 | convolution fusion | flops 1074003968 | bytes 4718592 | tf_op jit(solution)/shard_map/dot_general | solution.py:227
  273.3 4.3 %fusion.12 = bf16[512,512]{1,0:T(8,128)(2,1)} fusion(bf16[512,2048]{1,0:T(8,128)(2,1)} %all-gather.4.cloned.1.call-done, bf16[2048,3,512]{2,0,1:T(8,128)(2,1)} %param.14), kind=kOutput, calls=%fused_computation.15 | convolution fusion | flops 1074003968 | bytes 4718592 | tf_op jit(solution)/shard_map/dot_general | solution.py:227
  277.6 0.0 reduce-scatter.5.cloned.1.call-start
  277.6 3.7 fusion.18.q_ref
  281.3 13.3 %all-gather.8.cloned.1.call-done.v_ref = bf16[2048,512]{1,0:T(8,128)(2,1)} async-done(((bf16[512,512]{1,0:T(8,128)(2,1)}), bf16[2048,512]{1,0:T(8,128)(2,1)}) %all-gather.8.cloned.1.call-update) | async-done | bytes 2097168 | tf_op jit(solution)/shard_map/all_gather | solution.py:230
  294.7 24.1 %all-gather.6.cloned.1.call-done.k_ref = bf16[2048,512]{1,0:T(8,128)(2,1)} async-done(((bf16[512,512]{1,0:T(8,128)(2,1)}), bf16[2048,512]{1,0:T(8,128)(2,1)}) %all-gather.6.cloned.1.call-update) | async-done | bytes 2097168 | tf_op jit(solution)/shard_map/all_gather | solution.py:229
  318.8 1.6 copy-done.2
  320.4 1.6 copy-done.3
  322.0 9.5 %attend.1 = bf16[512,512]{1,0:T(8,128)(2,1)S(1)} custom-call(bf16[512,512]{1,0:T(8,128)(2,1)S(1)} %fusion.18.q_ref, bf16[2048,512]{1,0:T(8,128)(2,1)S(1)} %copy-done.3, bf16[2048,512]{1,0:T(8,128)(2,1)S(1)} %copy-done.2), custom_call_target="tpu_custom_call" | custom-call | tf_op jit(solution)/shard_map/attend/pallas_call | solution.py:160
  331.5 2.6 convolution_convert_fusion
  334.1 44.0 %reduce-scatter.5.cloned.1.call-done = bf16[128,2048]{1,0:T(8,128)(2,1)} async-done(((bf16[512,2048]{1,0:T(8,128)(2,1)}), bf16[128,2048]{1,0:T(8,128)(2,1)}) %reduce-scatter.5.cloned.1.call-update) | async-done | bytes 524304 | tf_op jit(solution)/shard_map/reduce_scatter | solution.py:233
  378.1 2.0 fusion.24
  (19 shorter events, 0.2 us)
Async XLA Ops:
  6.5 324.9 %copy-start = (bf16[512,2048]{1,0:T(8,128)(2,1)S(1)}, bf16[512,2048]{1,0:T(8,128)(2,1)}, u32[]{:S(2)}) copy-start(bf16[512,2048]{1,0:T(8,128)(2,1)} %param.15) | copy-start | bytes 6291460
  10.9 8.6 %copy-start.6 = (s32[256,2]{0,1:T(2,128)S(1)}, s32[256,2]{0,1:T(2,128)}, u32[]{:S(2)}) copy-start(s32[256,2]{0,1:T(2,128)} %param.11) | copy-start | bytes 6148
  12.1 23.9 %all-to-all-start = ((bf16[16,2,69,128]{3,1,2,0:T(2,128)(2,1)}), bf16[16,2,69,128]{3,1,2,0:T(2,128)(2,1)S(1)}, u32[]{:S(2)}, u32[]{:S(2)}) async-start(bf16[16,2,69,128]{3,1,2,0:T(2,128)(2,1)} %copy.16), calls=%async_computation | async-start | bytes 1130496 | tf_op jit(solution)/shard_map/all_to_all | solution.py:212
  19.4 200.8 %reduce-scatter.3.cloned.1.call-start = ((), (), s32[]{:S(2)}) async-start(), calls=%async_computation.4 | async-start | bytes 2621440 | tf_op jit(solution)/shard_map/reduce_scatter | solution.py:220
  176.0 1.3 copy-start.1
  177.4 44.1 %copy-start.5 = (f32[2048]{0:T(1024)S(1)}, f32[2048]{0:T(1024)}, u32[]{:S(2)}) copy-start(f32[2048]{0:T(1024)} %param.13) | copy-start | bytes 24580
  177.4 91.5 %all-gather.4.cloned.1.call-start = ((), (), s32[]{:S(2)}) async-start(), calls=%async_computation.5 | async-start | bytes 2621440 | tf_op jit(solution)/shard_map/all_gather | solution.py:224
  223.5 71.2 %all-gather.8.cloned.1.call-start = ((), (), s32[]{:S(2)}) async-start(), calls=%async_computation.7 | async-start | bytes 2621440 | tf_op jit(solution)/shard_map/all_gather | solution.py:230
  273.2 45.6 %all-gather.6.cloned.1.call-start = ((), (), s32[]{:S(2)}) async-start(), calls=%async_computation.6 | async-start | bytes 2621440 | tf_op jit(solution)/shard_map/all_gather | solution.py:229
  277.6 100.6 %reduce-scatter.5.cloned.1.call-start = ((), (), s32[]{:S(2)}) async-start(), calls=%async_computation.8 | async-start | bytes 2621440 | tf_op jit(solution)/shard_map/reduce_scatter | solution.py:233
  318.8 1.6 copy-start.2
  320.4 1.6 copy-start.3
  334.1 44.1 %copy-start.4 = (bf16[128,2048]{1,0:T(8,128)(2,1)S(1)}, bf16[128,2048]{1,0:T(8,128)(2,1)}, u32[]{:S(2)}) copy-start(bf16[128,2048]{1,0:T(8,128)(2,1)} %reduce-scatter.3.cloned.1.call-done) | copy-start | bytes 1572868
Sparse Core Ops, SparseCore 0:
  177.5 42.6 reduce-scatter.2
  223.6 45.2 all-gather.3
  273.3 21.2 all-gather.7
  296.2 22.5 all-gather.5
  334.2 43.8 reduce-scatter.4

commit v2 on v1

--- a/solution.py
+++ b/solution.py
@@ -84,63 +84,268 @@
     )(slots, arrived, tiles)
 
 
-def embed_kernel(pairs, per, channels, px_ref, w_ref, out_ref, lhs, acc):
-    step = pl.program_id(0)
-    last = pl.num_programs(0) - 1
-    senders, _, toks, _ = px_ref.shape
-    width = out_ref.shape[1]
-    tile = 512
-
-    @pl.when(step == 0)
-    def _():
-        acc[...] = jnp.zeros_like(acc)
-
-    def multiply(count, rows):
-        for s in range(senders):
-            for j in range(count):
-                lhs[s * toks : (s + 1) * toks, j * LANES : (j + 1) * LANES] = px_ref[s, j]
-
-        @pl.loop(0, width // tile)
+def peer_of(axis, far):
+    me = lax.axis_index(axis)
+    if far == 1:
+        return me + 1 - 2 * lax.rem(me, 2)
+    if far == 2:
+        return lax.rem(me + 2, 4)
+    return 3 - me
+
+
+def greet(pairs_of):
+    barrier = pltpu.get_barrier_semaphore()
+    for axis, far in pairs_of:
+        pl.semaphore_signal(
+            barrier,
+            inc=1,
+            device_id={axis: peer_of(axis, far)},
+            device_id_type=pl.DeviceIdType.MESH,
+        )
+    pl.semaphore_wait(barrier, len(pairs_of))
+
+
+def push(src, dst, send, recv, axis, far):
+    return pltpu.make_async_remote_copy(
+        src_ref=src,
+        dst_ref=dst,
+        send_sem=send,
+        recv_sem=recv,
+        device_id={axis: peer_of(axis, far)},
+        device_id_type=pl.DeviceIdType.MESH,
+    )
+
+
+def embed_kernel(
+    channels,
+    px_ref,
+    w_ref,
+    out_ref,
+    recv,
+    w,
+    lhs,
+    part,
+    got,
+    total,
+    local_sem,
+    send_sem,
+    recv_sem,
+    part_send,
+    part_recv,
+):
+    _, pairs, toks, _ = recv.shape
+    tiles, _, tile = total.shape
+    me = lax.axis_index("tensor")
+    load = pltpu.make_async_copy(w_ref, w.at[pl.ds(0, channels)], local_sem.at[0])
+    load.start()
+    own = pltpu.make_async_copy(px_ref.at[me], recv.at[0], local_sem.at[1])
+    own.start()
+    if channels < 2 * pairs:
+        w[channels:] = jnp.zeros((2 * pairs - channels,) + w.shape[1:], w.dtype)
+    greet([("tensor", far) for far in (1, 2, 3)])
+    moves = [
+        push(
+            px_ref.at[peer_of("tensor", far)],
+            recv.at[far],
+            send_sem.at[far - 1],
+            recv_sem.at[far - 1],
+            "tensor",
+            far,
+        )
+        for far in (1, 2, 3)
+    ]
+    moves[1].start()
+    moves[0].start()
+
+    def back(far, i):
+        return push(
+            part.at[far - 1, i],
+            got.at[far - 1, i],
+            part_send.at[far - 1, i],
+            part_recv.at[far - 1, i],
+            "tensor",
+            far,
+        )
+
+    def multiply(far):
+        @pl.loop(0, pairs)
+        def _(j):
+            lhs[:, pl.ds(pl.multiple_of(j * LANES, LANES), LANES)] = recv[far, j]
+
+        @pl.loop(0, tiles)
         def _(i):
             cols = pl.ds(pl.multiple_of(i * tile, tile), tile)
-            w = w_ref[: 2 * count, :, cols].reshape(count * LANES, tile)
-            if rows < count * LANES:
-                place = lax.broadcasted_iota(jnp.int32, w.shape, 0)
-                w = jnp.where(place < rows, w, jnp.zeros_like(w))
-            acc[:, cols] += jnp.dot(
-                lhs[:, : count * LANES], w, preferred_element_type=jnp.float32
-            )
-
-    @pl.when(step < last)
-    def _():
-        multiply(per, per * LANES)
-
-    @pl.when(step == last)
-    def _():
-        before = (pairs - 1) // per * per
-        multiply(pairs - before, (channels - 2 * before) * (LANES // 2))
-        out_ref[...] = acc[...].astype(out_ref.dtype)
-
-
-def embed(pixels, weight, per=6):
+            rhs = w[:, :, cols].reshape(pairs * LANES, tile)
+            summed = jnp.dot(lhs[...], rhs, preferred_element_type=jnp.float32)
+            if far == 0:
+                total[i] = summed
+            else:
+                part[far - 1, i] = summed.astype(part.dtype)
+                back(far, i).start()
+
+    own.wait()
+    load.wait()
+    multiply(0)
+    moves[1].wait_send()
+    moves[2].start()
+    moves[1].wait_recv()
+    multiply(2)
+    moves[0].wait()
+    multiply(1)
+    moves[2].wait()
+    multiply(3)
+
+    @pl.loop(0, tiles)
+    def _(i):
+        summed = total[i]
+        for far in (1, 2, 3):
+            back(far, i).wait()
+            summed += got[far - 1, i].astype(jnp.float32)
+        cols = pl.ds(pl.multiple_of(i * tile, tile), tile)
+        out_ref[:, cols] = summed.astype(out_ref.dtype)
+
+
+def embed(pixels, weight, tile=512):
     senders, pairs, toks, _ = pixels.shape
     channels, sub_pix, width = weight.shape
+    tiles = width // tile
     return pl.pallas_call(
-        functools.partial(embed_kernel, pairs, per, channels),
-        out_shape=jax.ShapeDtypeStruct((senders * toks, width), jnp.bfloat16),
-        grid=(pl.cdiv(pairs, per),),
-        in_specs=[
-            pl.BlockSpec((senders, per, toks, LANES), lambda i: (0, i, 0, 0)),
-            pl.BlockSpec((2 * per, sub_pix, width), lambda i: (i, 0, 0)),
+        functools.partial(embed_kernel, channels),
+        out_shape=jax.ShapeDtypeStruct((toks, width), jnp.bfloat16),
+        in_specs=[pl.BlockSpec(memory_space=pl.ANY)] * 2,
+        out_specs=pl.BlockSpec(memory_space=pltpu.VMEM),
+        scratch_shapes=[
+            pltpu.VMEM(pixels.shape, jnp.bfloat16),
+            pltpu.VMEM((2 * pairs, sub_pix, width), jnp.bfloat16),
+            pltpu.VMEM((toks, pairs * LANES), jnp.bfloat16),
+            pltpu.VMEM((3, tiles, toks, tile), jnp.bfloat16),
+            pltpu.VMEM((3, tiles, toks, tile), jnp.bfloat16),
+            pltpu.VMEM((tiles, toks, tile), jnp.float32),
+            pltpu.SemaphoreType.DMA((2,)),
+            pltpu.SemaphoreType.DMA((3,)),
+            pltpu.SemaphoreType.DMA((3,)),
+            pltpu.SemaphoreType.DMA((3, tiles)),
+            pltpu.SemaphoreType.DMA((3, tiles)),
         ],
-        out_specs=pl.BlockSpec((senders * toks, width), lambda i: (0, 0)),
-        scratch_shapes=[
-            pltpu.VMEM((senders * toks, per * LANES), jnp.bfloat16),
-            pltpu.VMEM((senders * toks, width), jnp.float32),
-        ],
-        compiler_params=pltpu.CompilerParams(vmem_limit_bytes=48 * MIB),
+        compiler_params=pltpu.CompilerParams(
+            collective_id=0, has_side_effects=True, vmem_limit_bytes=50 * MIB
+        ),
         name="embed",
     )(pixels, weight)
+
+
+def project_kernel(
+    x_ref,
+    gain_ref,
+    w_ref,
+    q_ref,
+    k_ref,
+    v_ref,
+    rows,
+    w,
+    load_sem,
+    row_send,
+    row_recv,
+    key_send,
+    key_recv,
+    value_send,
+    value_recv,
+):
+    load = pltpu.make_async_copy(w_ref, w, load_sem)
+    load.start()
+    values = x_ref[...].astype(jnp.float32)
+    factor = lax.rsqrt(jnp.mean(values * values, axis=-1, keepdims=True) + EPS)
+    rows[0] = (values * factor * gain_ref[...]).astype(jnp.bfloat16)
+    toks = rows.shape[1]
+    greet([("tensor", 1), ("tensor", 2), ("patch", 1), ("patch", 2)])
+
+    def row_move(src, dst, far):
+        return push(rows.at[src], rows.at[dst], row_send.at[dst], row_recv.at[dst], "tensor", far)
+
+    across = row_move(0, 2, 2)
+    beside = row_move(0, 1, 1)
+    relay = row_move(2, 3, 1)
+    across.start()
+    beside.start()
+    load.wait()
+
+    def cross(block, src, dst, far):
+        return [
+            push(
+                ref.at[src, block],
+                ref.at[dst, block],
+                sent.at[dst, block],
+                came.at[dst, block],
+                "patch",
+                far,
+            )
+            for ref, sent, came in (
+                (k_ref, key_send, key_recv),
+                (v_ref, value_send, value_recv),
+            )
+        ]
+
+    def project(block):
+        x = rows[block]
+        k_ref[0, block] = jnp.dot(x, w[1], preferred_element_type=jnp.float32).astype(jnp.bfloat16)
+        v_ref[0, block] = jnp.dot(x, w[2], preferred_element_type=jnp.float32).astype(jnp.bfloat16)
+        for copy in cross(block, 0, 2, 2) + cross(block, 0, 1, 1):
+            copy.start()
+        query = jnp.dot(x, w[0], preferred_element_type=jnp.float32) * HD ** (-0.5)
+        place = lax.axis_index("tensor") if block == 0 else peer_of("tensor", block)
+        q_ref[pl.ds(pl.multiple_of(place * toks, toks), toks), :] = query.astype(jnp.bfloat16)
+
+    project(0)
+    across.wait_recv()
+    relay.start()
+    project(2)
+    beside.wait_recv()
+    project(1)
+    for block in (0, 2):
+        for copy in cross(block, 0, 2, 2):
+            copy.wait_recv()
+        for copy in cross(block, 2, 3, 1):
+            copy.start()
+    relay.wait_recv()
+    project(3)
+    for block in (1, 3):
+        for copy in cross(block, 0, 2, 2):
+            copy.wait_recv()
+        for copy in cross(block, 2, 3, 1):
+            copy.start()
+    for block in range(4):
+        for copy in cross(block, 0, 1, 1) + cross(block, 2, 3, 1):
+            copy.wait()
+        for copy in cross(block, 0, 2, 2):
+            copy.wait_send()
+    for copy in (across, beside, relay):
+        copy.wait_send()
+
+
+def project_all(x, gain, weight):
+    toks, width = x.shape
+    heads_width = weight.shape[2]
+    kept = jax.ShapeDtypeStruct((4, 4, toks, heads_width), jnp.bfloat16)
+    in_vmem = pl.BlockSpec(memory_space=pltpu.VMEM)
+    query, keys, values = pl.pallas_call(
+        project_kernel,
+        out_shape=(jax.ShapeDtypeStruct((4 * toks, heads_width), jnp.bfloat16), kept, kept),
+        in_specs=[in_vmem, in_vmem, pl.BlockSpec(memory_space=pl.ANY)],
+        out_specs=(in_vmem, in_vmem, in_vmem),
+        scratch_shapes=[
+            pltpu.VMEM((4, toks, width), jnp.bfloat16),
+            pltpu.VMEM(weight.shape, jnp.bfloat16),
+            pltpu.SemaphoreType.DMA,
+            pltpu.SemaphoreType.DMA((4,)),
+            pltpu.SemaphoreType.DMA((4,)),
+        ]
+        + [pltpu.SemaphoreType.DMA((4, 4))] * 4,
+        compiler_params=pltpu.CompilerParams(
+            collective_id=1, has_side_effects=True, vmem_limit_bytes=40 * MIB
+        ),
+        name="project_all",
+    )(x, gain, weight)
+    return query, keys.reshape(-1, heads_width), values.reshape(-1, heads_width)
 
 
 def attend_kernel(q_ref, k_ref, v_ref, out_ref):
@@ -190,6 +395,20 @@
     return jnp.einsum(
         "ctq,cqd->td", pixels, emb_weight, preferred_element_type=jnp.float32
     ).astype(jnp.bfloat16)
+
+
+def general_project(own_rows, norm_gain, attention_in):
+    values_f = own_rows.astype(jnp.float32)
+    factor = lax.rsqrt(jnp.mean(values_f * values_f, axis=-1, keepdims=True) + EPS)
+    normed = (values_f * factor * norm_gain).astype(jnp.bfloat16)
+    normed = lax.all_gather(normed, "tensor", axis=0, tiled=True)
+
+    def project(part):
+        return jnp.dot(normed, attention_in[:, part], preferred_element_type=jnp.float32)
+
+    keys = lax.all_gather(project(1).astype(jnp.bfloat16), "patch", axis=0, tiled=True)
+    values = lax.all_gather(project(2).astype(jnp.bfloat16), "patch", axis=0, tiled=True)
+    return (project(0) * HD ** (-0.5)).astype(jnp.bfloat16), keys, values
 
 
 def on_device(
@@ -211,24 +430,21 @@
     )
     arrived = lax.all_to_all(payload, ("patch", "tensor"), split_axis=0, concat_axis=0, tiled=True)
     arrived = arrived.reshape(peers * slots, channels, cell_rows)
-    if 2 * emb_weight.shape[1] == LANES and intersection_tiles.shape[0] % 32 == 0:
+    if (
+        2 * emb_weight.shape[1] == LANES
+        and n_tensor == 4
+        and lax.axis_size("patch") == 4
+        and intersection_tiles.shape[0] % 32 == 0
+    ):
         pixels = regrid(arrived, intersection_tiles, intersection.reshape(-1))
-        pixels = lax.all_to_all(pixels, "tensor", split_axis=0, concat_axis=0, tiled=True)
-        partial = embed(pixels, emb_weight)
+        own_rows = embed(pixels, emb_weight)
+        query, keys, values = project_all(
+            own_rows, norm_gain[None, :], jnp.transpose(attention_in, (1, 0, 2))
+        )
     else:
         partial = general_embed(arrived, intersection_tiles, intersection, emb_weight, n_tensor)
-    own_rows = lax.psum_scatter(partial, "tensor", scatter_dimension=0, tiled=True)
-    values_f = own_rows.astype(jnp.float32)
-    factor = lax.rsqrt(jnp.mean(values_f * values_f, axis=-1, keepdims=True) + EPS)
-    normed = (values_f * factor * norm_gain).astype(jnp.bfloat16)
-    normed = lax.all_gather(normed, "tensor", axis=0, tiled=True)
-
-    def project(part):
-        return jnp.dot(normed, attention_in[:, part], preferred_element_type=jnp.float32)
-
-    keys = lax.all_gather(project(1).astype(jnp.bfloat16), "patch", axis=0, tiled=True)
-    values = lax.all_gather(project(2).astype(jnp.bfloat16), "patch", axis=0, tiled=True)
-    query = (project(0) * HD ** (-0.5)).astype(jnp.bfloat16)
+        own_rows = lax.psum_scatter(partial, "tensor", scatter_dimension=0, tiled=True)
+        query, keys, values = general_project(own_rows, norm_gain, attention_in)
     heads_out = attend(query, keys, values)
     mixing = lax.psum_scatter(
         jnp.dot(heads_out, attention_out, preferred_element_type=jnp.float32).astype(jnp.bfloat16),
@@ -236,7 +452,7 @@
         scatter_dimension=0,
         tiled=True,
     ).astype(jnp.float32)
-    return (values_f + mixing).astype(jnp.bfloat16)
+    return (own_rows.astype(jnp.float32) + mixing).astype(jnp.bfloat16)
 
 
 def solution(mesh):

time: 387 us -> 315 us (0.81)
  Pallas kernels: 44.3 us -> 221 us
  waiting for transfers between devices: 186 us -> 60.4 us
  blocking collectives: 105 us -> 0 us
  matrix products: 14.8 us -> 2.59 us
    pallas_call x1 -> x2, Pallas kernels: 17.6 us -> 194 us  [the longest x1 137 us: embed(): pl.pallas_call(functools.partial(embed_kernel, channels), out_shape=jax.S...]
    all_to_all x1 -> x0, blocking collectives: 105 us -> none  [on_device(): lax.all_to_all(pixels, 'tensor', split_axis=0, concat_axis=0, tiled=True)]
    all_gather x3 -> x0, waiting for transfers between devices: 82.8 us -> none  [the longest x1 45.4 us: on_device(): normed = lax.all_gather(normed, 'tensor', axis=0, tiled=True)]
    reduce_scatter x1 -> x0, waiting for transfers between devices: 42.8 us -> none  [on_device(): lax.psum_scatter(partial, 'tensor', scatter_dimension=0, tiled=True)]
    dot_general x3 -> x0, matrix products: 12.3 us -> none  [project(): jnp.dot(normed, attention_in[:, part], preferred_element_type=jnp.float32)]
  transfers between devices with their start and end apart: 6 -> 2, of which waited for: 6 -> 2; matrix products, arithmetic and copies ran while one was open for 2% -> 0% of each run, Pallas kernels for 0% -> 0%
where the time goes in v2:
time: 315 us; the launch traced here: 314 us
  Pallas kernels  221 us (70%)
  waiting for transfers between devices  60.4 us (19%)
  between operations  13.5 us (4%)
  local copies, waits for them, and re-layouts  7.95 us (3%)
  starting transfers between devices  7.4 us (2%)
    pallas_call x1, Pallas kernels, embed(): pl.pallas_call(functools.partial(embed_kernel, channels), out_shape=jax.S...  137 us
    pallas_call x1, Pallas kernels, project_all(): pl.pallas_call(project_kernel, out_shape=(jax.ShapeDtypeStruct((4 * toks,...  57 us
    reduce_scatter x1, waiting for transfers between devices, on_device(): lax.psum_scatter(jnp.dot(heads_out, attention_out, preferred_element_type...  44.2 us
    pallas_call x1, Pallas kernels, regrid(): pl.pallas_call(functools.partial(regrid_kernel, channels, toks), out_shap...  17.5 us
    all_to_all x1, waiting for transfers between devices, on_device(): lax.all_to_all(payload, ('patch', 'tensor'), split_axis=0, concat_axis=0,...  16.2 us
    pallas_call x1, Pallas kernels, attend(): pl.pallas_call(attend_kernel, out_shape=jax.ShapeDtypeStruct(query.shape,...  9.52 us
    all_to_all x1, starting transfers between devices, on_device(): lax.all_to_all(payload, ('patch', 'tensor'), split_axis=0, concat_axis=0,...  7.36 us
  transfers between devices with their start and end apart: 2, of which 2 were waited for; matrix products, arithmetic and copies ran while one was open for 0% of the time, Pallas kernels for 0%

profile of v2, /device:TPU:0, one launch (start us, length us, event | category | flops | bytes accessed | tf_op | source)
XLA Modules:
  0.0 314.4 jit_solution(14554407382415916104)
XLA Ops:
  6.5 0.0 copy-start
  6.5 0.9 copy.15
  7.4 0.1 reshape.24
  7.5 3.3 %gather_fusion = bf16[32,69,128]{2,0,1:T(8,128)(2,1)S(1)} fusion(bf16[256,69,128]{2,0,1:T(8,128)(2,1)} %param.8, s32[1024]{0:T(1024)S(1)} %pad_clamp_fusion), kind=kCustom, calls=%fused_computation | custom fusion | bytes 1130624 | tf_op jit(solution)/shard_map/jit(_take)/gather | solution.py:428
  10.9 0.0 copy-start.3
  10.9 1.2 copy.16
  12.1 7.4 %all-to-all-start = ((bf16[16,2,69,128]{3,1,2,0:T(2,128)(2,1)}), bf16[16,2,69,128]{3,1,2,0:T(2,128)(2,1)S(1)}, u32[]{:S(2)}, u32[]{:S(2)}) async-start(bf16[16,2,69,128]{3,1,2,0:T(2,128)(2,1)} %copy.16), calls=%async_computation | async-start | bytes 1130496 | tf_op jit(solution)/shard_map/all_to_all | solution.py:431
  19.4 0.0 reduce-scatter.2.cloned.1.call-start
  19.5 0.0 copy-done.3
  19.5 0.1 copy.14
  19.6 0.1 reshape.17.slot_ref
  19.8 16.2 %all-to-all-done = bf16[16,2,69,128]{3,1,2,0:T(2,128)(2,1)S(1)} async-done(((bf16[16,2,69,128]{3,1,2,0:T(2,128)(2,1)}), bf16[16,2,69,128]{3,1,2,0:T(2,128)(2,1)S(1)}, u32[]{:S(2)}, u32[]{:S(2)}) %all-to-all-start) | async-done | bytes 565280 | tf_op jit(solution)/shard_map/all_to_all | solution.py:431
  36.0 0.1 copy.17
  36.1 0.0 slice-start
  36.1 17.5 %regrid.1.px_ref = bf16[4,35,128,128]{3,2,1,0:T(8,128)(2,1)S(1)} custom-call(s32[512]{0:T(512)S(1)} %reshape.17.slot_ref, bf16[32,69,128]{2,1,0:T(8,128)(2,1)S(1)} %bitcast.11, bf16[256,2,128,128]{3,2,1,0:T(8,128)(2,1)} %tiles_ref.1), custom_call_target="tpu_custom_call" | custom-call | tf_op jit(solution)/shard_map/regrid/pallas_call | solution.py:66
  53.6 0.0 copy-start.1
  53.6 2.1 copy-done.1
  55.7 0.0 slice-start.1
  55.7 0.0 copy-start.2
  55.7 136.5 %embed.1.x_ref = bf16[128,2048]{1,0:T(8,128)(2,1)S(1)} custom-call(bf16[4,35,128,128]{3,2,1,0:T(8,128)(2,1)} %copy-done.1, bf16[69,64,2048]{2,1,0:T(8,128)(2,1)} %w_ref.1), custom_call_target="tpu_custom_call" | custom-call | tf_op jit(solution)/shard_map/embed/pallas_call | solution.py:212
  192.2 0.0 slice-done
  192.2 0.0 slice-done.1
  192.2 0.0 copy-done.2
  192.2 57.0 %project_all.1 = (bf16[512,512]{1,0:T(8,128)(2,1)S(1)}, bf16[4,4,128,512]{3,2,1,0:T(8,128)(2,1)S(1)}, bf16[4,4,128,512]{3,2,1,0:T(8,128)(2,1)S(1)}) custom-call(bf16[128,2048]{1,0:T(8,128)(2,1)S(1)} %embed.1.x_ref, f32[1,2048]{1,0:T(1,128)S(1)} %bitcast.14, bf16[3,2048,512]{2,1,0:T(8,128)(2,1)S(1)} %bitcast.10), custom_call_target="tpu_custom_call" | custom-call | tf_op jit(solution)/shard_map/project_all/pallas_call | solution.py:330
  249.2 9.5 %attend.1 = bf16[512,512]{1,0:T(8,128)(2,1)S(1)} custom-call(bf16[512,512]{1,0:T(8,128)(2,1)S(1)} %get-tuple-element.8.q_ref, bf16[2048,512]{1,0:T(8,128)(2,1)S(1)} %bitcast.12, bf16[2048,512]{1,0:T(8,128)(2,1)S(1)} %bitcast.13), custom_call_target="tpu_custom_call" | custom-call | tf_op jit(solution)/shard_map/attend/pallas_call | solution.py:365
  258.8 0.0 copy-done
  258.8 2.6 convolution_convert_fusion
  261.4 0.0 reduce-scatter.2.cloned.1.call-update
  261.4 44.2 %reduce-scatter.2.cloned.1.call-done = bf16[128,2048]{1,0:T(8,128)(2,1)} async-done(((bf16[512,2048]{1,0:T(8,128)(2,1)}), bf16[128,2048]{1,0:T(8,128)(2,1)}) %reduce-scatter.2.cloned.1.call-update) | async-done | bytes 524304 | tf_op jit(solution)/shard_map/reduce_scatter | solution.py:449
  305.6 2.0 add_convert_fusion
  (2 shorter events, 0.0 us)
Async XLA Ops:
  6.5 252.2 %copy-start = (bf16[512,2048]{1,0:T(8,128)(2,1)S(1)}, bf16[512,2048]{1,0:T(8,128)(2,1)}, u32[]{:S(2)}) copy-start(bf16[512,2048]{1,0:T(8,128)(2,1)} %param.15) | copy-start | bytes 6291460
  10.9 8.6 %copy-start.3 = (s32[256,2]{0,1:T(2,128)S(1)}, s32[256,2]{0,1:T(2,128)}, u32[]{:S(2)}) copy-start(s32[256,2]{0,1:T(2,128)} %param.11) | copy-start | bytes 6148
  12.1 23.9 %all-to-all-start = ((bf16[16,2,69,128]{3,1,2,0:T(2,128)(2,1)}), bf16[16,2,69,128]{3,1,2,0:T(2,128)(2,1)S(1)}, u32[]{:S(2)}, u32[]{:S(2)}) async-start(bf16[16,2,69,128]{3,1,2,0:T(2,128)(2,1)} %copy.16), calls=%async_computation | async-start | bytes 1130496 | tf_op jit(solution)/shard_map/all_to_all | solution.py:431
  19.4 286.1 %reduce-scatter.2.cloned.1.call-start = ((), (), s32[]{:S(2)}) async-start(), calls=%async_computation.2 | async-start | bytes 2621440 | tf_op jit(solution)/shard_map/reduce_scatter | solution.py:449
  36.1 156.1 %slice-start = ((s8[6291456]{0:T(1024)(128)(4,1)}), s8[4194304]{0:T(1024)(128)(4,1)S(1)}, s32[]{:S(2)}) async-start(s8[6291456]{0:T(1024)(128)(4,1)} %bitcast.8), calls=%async_computation.3 | async-start | bytes 8388608
  53.6 2.1 copy-start.1
  55.7 136.5 %slice-start.1 = ((s8[6291456]{0:T(1024)(128)(4,1)}), s8[2097152]{0:T(1024)(128)(4,1)S(1)}, s32[]{:S(2)}) async-start(s8[6291456]{0:T(1024)(128)(4,1)} %bitcast.8), calls=%async_computation.4 | async-start | bytes 4194304
  55.7 136.5 %copy-start.2 = (f32[2048]{0:T(1024)S(1)}, f32[2048]{0:T(1024)}, u32[]{:S(2)}) copy-start(f32[2048]{0:T(1024)} %param.13) | copy-start | bytes 24580
Sparse Core Ops, SparseCore 0:
  261.5 44.0 reduce-scatter.1

commit v3 on v2

--- a/solution.py
+++ b/solution.py
@@ -47,7 +47,7 @@
             rhs = tiles_ref[block].reshape(2 * tiles_ref.shape[2], LANES)
             numer = jnp.dot(lhs, rhs, preferred_element_type=jnp.float32)
             area = numer[pairs : pairs + 1]
-            value = numer / area
+            value = numer * (1.0 / area)
             even, odd = value[:half], value[half:]
             first = jnp.where(low, even, pltpu.roll(odd, LANES // 2, 1))
             second = jnp.where(low, pltpu.roll(even, LANES // 2, 1), odd)
@@ -154,7 +154,7 @@
         )
         for far in (1, 2, 3)
     ]
-    moves[1].start()
+    moves[2].start()
     moves[0].start()
 
     def back(far, i):
@@ -164,7 +164,7 @@
             part_send.at[far - 1, i],
             part_recv.at[far - 1, i],
             "tensor",
-            far,
+            2 if far == 2 else 1,
         )
 
     def multiply(far):
@@ -180,25 +180,29 @@
             if far == 0:
                 total[i] = summed
             else:
+                if far == 2:
+                    back(3, i).wait_recv()
+                    summed += got[2, i].astype(jnp.float32)
                 part[far - 1, i] = summed.astype(part.dtype)
                 back(far, i).start()
 
     own.wait()
     load.wait()
     multiply(0)
-    moves[1].wait_send()
-    moves[2].start()
-    moves[1].wait_recv()
-    multiply(2)
+    moves[2].wait_send()
+    moves[1].start()
+    moves[2].wait_recv()
+    multiply(3)
     moves[0].wait()
     multiply(1)
-    moves[2].wait()
-    multiply(3)
+    moves[1].wait()
+    multiply(2)
 
     @pl.loop(0, tiles)
     def _(i):
+        back(3, i).wait_send()
         summed = total[i]
-        for far in (1, 2, 3):
+        for far in (1, 2):
             back(far, i).wait()
             summed += got[far - 1, i].astype(jnp.float32)
         cols = pl.ds(pl.multiple_of(i * tile, tile), tile)
@@ -348,15 +352,97 @@
     return query, keys.reshape(-1, heads_width), values.reshape(-1, heads_width)
 
 
-def attend_kernel(q_ref, k_ref, v_ref, out_ref):
+def attend_rows(query, keys, values):
     scores = lax.dot_general(
-        q_ref[...], k_ref[...], (((1,), (1,)), ((), ())), preferred_element_type=jnp.float32
+        query, keys, (((1,), (1,)), ((), ())), preferred_element_type=jnp.float32
     )
     highest = jnp.max(scores, axis=-1, keepdims=True)
     expo = jnp.exp(scores - highest)
     denom = jnp.sum(expo, axis=-1, keepdims=True)
-    summed = jnp.dot(expo.astype(jnp.bfloat16), v_ref[...], preferred_element_type=jnp.float32)
-    out_ref[...] = (summed / denom).astype(jnp.bfloat16)
+    summed = jnp.dot(expo.astype(jnp.bfloat16), values, preferred_element_type=jnp.float32)
+    return (summed / denom).astype(jnp.bfloat16)
+
+
+def attend_kernel(q_ref, k_ref, v_ref, out_ref):
+    out_ref[...] = attend_rows(q_ref[...], k_ref[...], v_ref[...])
+
+
+def mix_kernel(
+    q_ref, k_ref, v_ref, w_ref, x_ref, out_ref, heads, total, part, got, send_sem, recv_sem
+):
+    _, tiles, toks, tile = part.shape
+
+    def back(far, i):
+        return push(
+            part.at[far - 1, i],
+            got.at[far - 1, i],
+            send_sem.at[far - 1, i],
+            recv_sem.at[far - 1, i],
+            "tensor",
+            2 if far == 2 else 1,
+        )
+
+    def attended(far):
+        place = lax.axis_index("tensor") if far == 0 else peer_of("tensor", far)
+        rows = pl.ds(pl.multiple_of(place * toks, toks), toks)
+        for head in range(heads.shape[1] // HD):
+            lanes = slice(head * HD, (head + 1) * HD)
+            heads[:, lanes] = attend_rows(q_ref[rows, lanes], k_ref[:, lanes], v_ref[:, lanes])
+
+    def mixed(i):
+        cols = slice(i * tile, (i + 1) * tile)
+        return jnp.dot(heads[...], w_ref[:, cols], preferred_element_type=jnp.float32)
+
+    greet([("tensor", 1), ("tensor", 2)])
+    attended(3)
+    for i in range(tiles):
+        part[2, i] = mixed(i).astype(part.dtype)
+        back(3, i).start()
+    attended(2)
+    for i in range(tiles):
+        total[i] = mixed(i)
+    attended(1)
+    for i in range(tiles):
+        part[0, i] = mixed(i).astype(part.dtype)
+    for i in range(tiles):
+        back(3, i).wait_recv()
+        part[1, i] = (total[i] + got[2, i].astype(jnp.float32)).astype(part.dtype)
+        back(2, i).start()
+        back(1, i).start()
+    attended(0)
+    for i in range(tiles):
+        total[i] = mixed(i)
+    for i in range(tiles):
+        back(3, i).wait_send()
+        back(1, i).wait()
+        back(2, i).wait()
+        cols = slice(i * tile, (i + 1) * tile)
+        summed = total[i] + got[0, i].astype(jnp.float32) + got[1, i].astype(jnp.float32)
+        out_ref[:, cols] = (x_ref[:, cols].astype(jnp.float32) + summed).astype(out_ref.dtype)
+
+
+def mix(query, keys, values, weight, x, tiles=4):
+    toks, width = x.shape
+    tile = width // tiles
+    in_vmem = pl.BlockSpec(memory_space=pltpu.VMEM)
+    return pl.pallas_call(
+        mix_kernel,
+        out_shape=jax.ShapeDtypeStruct(x.shape, jnp.bfloat16),
+        in_specs=[in_vmem] * 5,
+        out_specs=in_vmem,
+        scratch_shapes=[
+            pltpu.VMEM((toks, query.shape[1]), jnp.bfloat16),
+            pltpu.VMEM((tiles, toks, tile), jnp.float32),
+            pltpu.VMEM((3, tiles, toks, tile), jnp.bfloat16),
+            pltpu.VMEM((3, tiles, toks, tile), jnp.bfloat16),
+            pltpu.SemaphoreType.DMA((3, tiles)),
+            pltpu.SemaphoreType.DMA((3, tiles)),
+        ],
+        compiler_params=pltpu.CompilerParams(
+            collective_id=2, has_side_effects=True, vmem_limit_bytes=40 * MIB
+        ),
+        name="mix",
+    )(query, keys, values, weight, x)
 
 
 def attend(query, keys, values, rows=256):
@@ -441,10 +527,10 @@
         query, keys, values = project_all(
             own_rows, norm_gain[None, :], jnp.transpose(attention_in, (1, 0, 2))
         )
-    else:
-        partial = general_embed(arrived, intersection_tiles, intersection, emb_weight, n_tensor)
-        own_rows = lax.psum_scatter(partial, "tensor", scatter_dimension=0, tiled=True)
-        query, keys, values = general_project(own_rows, norm_gain, attention_in)
+        return mix(query, keys, values, attention_out, own_rows)
+    partial = general_embed(arrived, intersection_tiles, intersection, emb_weight, n_tensor)
+    own_rows = lax.psum_scatter(partial, "tensor", scatter_dimension=0, tiled=True)
+    query, keys, values = general_project(own_rows, norm_gain, attention_in)
     heads_out = attend(query, keys, values)
     mixing = lax.psum_scatter(
         jnp.dot(heads_out, attention_out, preferred_element_type=jnp.float32).astype(jnp.bfloat16),

time: 315 us -> 263 us (0.83)
  waiting for transfers between devices: 60.4 us -> 16.3 us
  between operations: 13.5 us -> 0.15 us
  Pallas kernels: 221 us -> 230 us
    reduce_scatter x1 -> x0, waiting for transfers between devices: 44.2 us -> none  [on_device(): lax.psum_scatter(jnp.dot(heads_out, attention_out, preferred_element_type...]
    pallas_call x1, Pallas kernels: 9.52 us -> 39.4 us  [mix(): pl.pallas_call(mix_kernel, out_shape=jax.ShapeDtypeStruct(x.shape, jnp.bf...]
    pallas_call x1, Pallas kernels: 137 us -> 126 us  [embed(): pl.pallas_call(functools.partial(embed_kernel, channels), out_shape=jax.S...]
    pallas_call x1, Pallas kernels: 57 us -> 47.1 us  [project_all(): pl.pallas_call(project_kernel, out_shape=(jax.ShapeDtypeStruct((4 * toks,...]
  transfers between devices with their start and end apart: 2 -> 1, of which waited for: 2 -> 1; matrix products, arithmetic and copies ran while one was open for 0% -> 0% of each run, Pallas kernels for 0% -> 0%
where the time goes in v3:
time: 263 us; the launch traced here: 262 us
  Pallas kernels  230 us (87%)
  waiting for transfers between devices  16.3 us (6%)
  local copies, waits for them, and re-layouts  8.61 us (3%)
  starting transfers between devices  7.36 us (3%)
    pallas_call x1, Pallas kernels, embed(): pl.pallas_call(functools.partial(embed_kernel, channels), out_shape=jax.S...  126 us
    pallas_call x1, Pallas kernels, project_all(): pl.pallas_call(project_kernel, out_shape=(jax.ShapeDtypeStruct((4 * toks,...  47.1 us
    pallas_call x1, Pallas kernels, mix(): pl.pallas_call(mix_kernel, out_shape=jax.ShapeDtypeStruct(x.shape, jnp.bf...  39.4 us
    pallas_call x1, Pallas kernels, regrid(): pl.pallas_call(functools.partial(regrid_kernel, channels, toks), out_shap...  17.5 us
    all_to_all x1, waiting for transfers between devices, on_device(): lax.all_to_all(payload, ('patch', 'tensor'), split_axis=0, concat_axis=0,...  16.3 us
    all_to_all x1, starting transfers between devices, on_device(): lax.all_to_all(payload, ('patch', 'tensor'), split_axis=0, concat_axis=0,...  7.36 us
  transfers between devices with their start and end apart: 1, of which 1 were waited for; matrix products, arithmetic and copies ran while one was open for 0% of the time, Pallas kernels for 0%

profile of v3, /device:TPU:0, one launch (start us, length us, event | category | flops | bytes accessed | tf_op | source)
XLA Modules:
  0.0 262.4 jit_solution(9172491005903647377)
XLA Ops:
  0.0 0.0 copy-start.3
  0.0 0.8 copy.15
  0.8 0.1 reshape.24
  0.9 3.3 %gather_fusion = bf16[32,69,128]{2,0,1:T(8,128)(2,1)S(1)} fusion(bf16[256,69,128]{2,0,1:T(8,128)(2,1)} %param.8, s32[1024]{0:T(1024)S(1)} %pad_clamp_fusion), kind=kCustom, calls=%fused_computation | custom fusion | bytes 1130624 | tf_op jit(solution)/shard_map/jit(_take)/gather | solution.py:514
  4.2 1.2 copy.16
  5.4 7.4 %all-to-all-start = ((bf16[16,2,69,128]{3,1,2,0:T(2,128)(2,1)}), bf16[16,2,69,128]{3,1,2,0:T(2,128)(2,1)S(1)}, u32[]{:S(2)}, u32[]{:S(2)}) async-start(bf16[16,2,69,128]{3,1,2,0:T(2,128)(2,1)} %copy.16), calls=%async_computation | async-start | bytes 1130496 | tf_op jit(solution)/shard_map/all_to_all | solution.py:517
  12.8 0.0 copy-done.3
  12.8 0.1 copy.14
  12.9 0.1 reshape.17.slot_ref
  13.1 16.3 %all-to-all-done = bf16[16,2,69,128]{3,1,2,0:T(2,128)(2,1)S(1)} async-done(((bf16[16,2,69,128]{3,1,2,0:T(2,128)(2,1)}), bf16[16,2,69,128]{3,1,2,0:T(2,128)(2,1)S(1)}, u32[]{:S(2)}, u32[]{:S(2)}) %all-to-all-start) | async-done | bytes 565280 | tf_op jit(solution)/shard_map/all_to_all | solution.py:517
  29.3 0.1 copy.17
  29.4 0.0 slice-start
  29.4 17.5 %regrid.1.px_ref = bf16[4,35,128,128]{3,2,1,0:T(8,128)(2,1)S(1)} custom-call(s32[512]{0:T(512)S(1)} %reshape.17.slot_ref, bf16[32,69,128]{2,1,0:T(8,128)(2,1)S(1)} %bitcast.9, bf16[256,2,128,128]{3,2,1,0:T(8,128)(2,1)} %tiles_ref.1), custom_call_target="tpu_custom_call" | custom-call | tf_op jit(solution)/shard_map/regrid/pallas_call | solution.py:66
  46.9 0.0 copy-start
  46.9 2.1 copy-done
  49.0 0.0 slice-start.1
  49.0 0.0 copy-start.2
  49.0 126.0 %embed.1.x_ref = bf16[128,2048]{1,0:T(8,128)(2,1)S(1)} custom-call(bf16[4,35,128,128]{3,2,1,0:T(8,128)(2,1)} %copy-done, bf16[69,64,2048]{2,1,0:T(8,128)(2,1)} %w_ref.2), custom_call_target="tpu_custom_call" | custom-call | tf_op jit(solution)/shard_map/embed/pallas_call | solution.py:216
  175.1 0.0 copy-start.1
  175.1 0.0 slice-done
  175.1 0.0 slice-done.1
  175.1 0.0 copy-done.2
  175.1 47.1 %project_all.1 = (bf16[512,512]{1,0:T(8,128)(2,1)S(1)}, bf16[4,4,128,512]{3,2,1,0:T(8,128)(2,1)S(1)}, bf16[4,4,128,512]{3,2,1,0:T(8,128)(2,1)S(1)}) custom-call(bf16[128,2048]{1,0:T(8,128)(2,1)S(1)} %embed.1.x_ref, f32[1,2048]{1,0:T(1,128)S(1)} %bitcast.12, bf16[3,2048,512]{2,1,0:T(8,128)(2,1)S(1)} %bitcast.8), custom_call_target="tpu_custom_call" | custom-call | tf_op jit(solution)/shard_map/project_all/pallas_call | solution.py:334
  222.2 0.0 copy-done.1
  222.3 39.4 %mix.1 = bf16[128,2048]{1,0:T(8,128)(2,1)S(1)} custom-call(bf16[512,512]{1,0:T(8,128)(2,1)S(1)} %get-tuple-element.8.q_ref, bf16[2048,512]{1,0:T(8,128)(2,1)S(1)} %bitcast.10, bf16[2048,512]{1,0:T(8,128)(2,1)S(1)} %bitcast.11, bf16[512,2048]{1,0:T(8,128)(2,1)S(1)} %copy-done.1, bf16[128,2048]{1,0:T(8,128)(2,1)S(1)} %embed.1.x_ref), custom_call_target="tpu_custom_call" | custom-call | tf_op jit(solution)/shard_map/mix/pallas_call | solution.py:428
  261.6 0.8 copy.19
  (2 shorter events, 0.0 us)
Async XLA Ops:
  0.0 12.8 %copy-start.3 = (s32[256,2]{0,1:T(2,128)S(1)}, s32[256,2]{0,1:T(2,128)}, u32[]{:S(2)}) copy-start(s32[256,2]{0,1:T(2,128)} %param.11) | copy-start | bytes 6148
  5.4 23.9 %all-to-all-start = ((bf16[16,2,69,128]{3,1,2,0:T(2,128)(2,1)}), bf16[16,2,69,128]{3,1,2,0:T(2,128)(2,1)S(1)}, u32[]{:S(2)}, u32[]{:S(2)}) async-start(bf16[16,2,69,128]{3,1,2,0:T(2,128)(2,1)} %copy.16), calls=%async_computation | async-start | bytes 1130496 | tf_op jit(solution)/shard_map/all_to_all | solution.py:517
  29.4 145.7 %slice-start = ((s8[6291456]{0:T(1024)(128)(4,1)}), s8[4194304]{0:T(1024)(128)(4,1)S(1)}, s32[]{:S(2)}) async-start(s8[6291456]{0:T(1024)(128)(4,1)} %bitcast.6), calls=%async_computation.1 | async-start | bytes 8388608
  46.9 2.1 copy-start
  49.0 126.1 %slice-start.1 = ((s8[6291456]{0:T(1024)(128)(4,1)}), s8[2097152]{0:T(1024)(128)(4,1)S(1)}, s32[]{:S(2)}) async-start(s8[6291456]{0:T(1024)(128)(4,1)} %bitcast.6), calls=%async_computation.2 | async-start | bytes 4194304
  49.0 126.1 %copy-start.2 = (f32[2048]{0:T(1024)S(1)}, f32[2048]{0:T(1024)}, u32[]{:S(2)}) copy-start(f32[2048]{0:T(1024)} %param.13) | copy-start | bytes 24580
  175.1 47.2 %copy-start.1 = (bf16[512,2048]{1,0:T(8,128)(2,1)S(1)}, bf16[512,2048]{1,0:T(8,128)(2,1)}, u32[]{:S(2)}) copy-start(bf16[512,2048]{1,0:T(8,128)(2,1)} %w_ref.3) | copy-start | bytes 6291460

commit v4 on v3

--- a/solution.py
+++ b/solution.py
@@ -17,71 +17,44 @@
     return -(-value // unit) * unit
 
 
-def regrid_kernel(channels, toks, slot_ref, arrived_ref, tiles_ref, out_ref, ordered, stage):
+def order_channels(arrived_ref, ordered):
+    channels = arrived_ref.shape[1]
     pairs = (channels + 1) // 2
-    half = round_up(pairs + 1, 8)
-    step = pl.program_id(0)
-
-    @pl.when(step == 0)
-    def _():
-        row = lax.broadcasted_iota(jnp.int32, (2 * half, channels), 0)
-        col = lax.broadcasted_iota(jnp.int32, (2 * half, channels), 1)
-        wanted = jnp.where(row < half, 2 * row, 2 * (row - half) + 1)
-        order = jnp.where(wanted == col, 1.0, 0.0).astype(jnp.bfloat16)
-        ones = lax.broadcasted_iota(jnp.int32, (2 * half, LANES), 0) == pairs
-
-        @pl.loop(0, arrived_ref.shape[0])
-        def _(slot):
-            moved = jnp.dot(order, arrived_ref[slot], preferred_element_type=jnp.float32)
-            keep = lax.broadcasted_iota(jnp.int32, (2 * half, LANES), 0)
-            valid = ((keep < pairs) | ((keep >= half) & (keep < half + channels // 2)))
-            moved = jnp.where(valid, moved, 0.0)
-            ordered[slot] = jnp.where(ones, 1.0, moved).astype(jnp.bfloat16)
-
+    half = ordered.shape[1] // 2
+    row = lax.broadcasted_iota(jnp.int32, (2 * half, channels), 0)
+    col = lax.broadcasted_iota(jnp.int32, (2 * half, channels), 1)
+    wanted = jnp.where(row < half, 2 * row, 2 * (row - half) + 1)
+    order = jnp.where(wanted == col, 1.0, 0.0).astype(jnp.bfloat16)
+    place = lax.broadcasted_iota(jnp.int32, (2 * half, LANES), 0)
+    valid = (place < pairs) | ((place >= half) & (place < half + channels // 2))
+
+    @pl.loop(0, arrived_ref.shape[0])
+    def _(slot):
+        moved = jnp.dot(order, arrived_ref[slot], preferred_element_type=jnp.float32)
+        moved = jnp.where(valid, moved, jnp.where(place == pairs, 1.0, 0.0))
+        ordered[slot] = moved.astype(jnp.bfloat16)
+
+
+def regrid(step, slot_ref, ordered, tiles, stage):
+    half = ordered.shape[1] // 2
+    toks = tiles.shape[0] // 2
+    pairs = stage.shape[0] // (4 * toks)
     low = lax.broadcasted_iota(jnp.int32, (half, LANES), 1) < LANES // 2
     for tok in range(toks):
         for side in range(2):
             block = tok * 2 + side
             base = (step * toks * 2 + block) * 2
             lhs = jnp.concatenate([ordered[slot_ref[base]], ordered[slot_ref[base + 1]]], axis=1)
-            rhs = tiles_ref[block].reshape(2 * tiles_ref.shape[2], LANES)
+            rhs = tiles[block].reshape(2 * tiles.shape[2], LANES)
             numer = jnp.dot(lhs, rhs, preferred_element_type=jnp.float32)
-            area = numer[pairs : pairs + 1]
-            value = numer * (1.0 / area)
+            value = numer * (1.0 / numer[pairs : pairs + 1])
             even, odd = value[:half], value[half:]
             first = jnp.where(low, even, pltpu.roll(odd, LANES // 2, 1))
             second = jnp.where(low, pltpu.roll(even, LANES // 2, 1), odd)
             start = 2 * side * pairs * toks + tok
             stage[pl.ds(start, pairs, stride=toks), :] = first[:pairs]
             stage[pl.ds(start + pairs * toks, pairs, stride=toks), :] = second[:pairs]
-    out_ref[...] = stage[...].reshape(4, pairs, toks, LANES).astype(jnp.bfloat16)
-
-
-def regrid(arrived, tiles, slots, toks=16):
-    n_slots, channels, cells = arrived.shape
-    blocks = tiles.shape[0]
-    tok_local = blocks // 2
-    pairs = (channels + 1) // 2
-    half = round_up(pairs + 1, 8)
-    return pl.pallas_call(
-        functools.partial(regrid_kernel, channels, toks),
-        out_shape=jax.ShapeDtypeStruct((4, pairs, tok_local, LANES), jnp.bfloat16),
-        grid_spec=pltpu.PrefetchScalarGridSpec(
-            num_scalar_prefetch=1,
-            grid=(tok_local // toks,),
-            in_specs=[
-                pl.BlockSpec((n_slots, channels, cells), lambda i, s: (0, 0, 0)),
-                pl.BlockSpec((2 * toks,) + tiles.shape[1:], lambda i, s: (i, 0, 0, 0)),
-            ],
-            out_specs=pl.BlockSpec((4, pairs, toks, LANES), lambda i, s: (0, 0, i, 0)),
-            scratch_shapes=[
-                pltpu.VMEM((n_slots, 2 * half, cells), jnp.bfloat16),
-                pltpu.VMEM((4 * pairs * toks, LANES), jnp.float32),
-            ],
-        ),
-        compiler_params=pltpu.CompilerParams(vmem_limit_bytes=40 * MIB),
-        name="regrid",
-    )(slots, arrived, tiles)
+    return stage[...].reshape(4, pairs, toks, LANES).astype(jnp.bfloat16)
 
 
 def peer_of(axis, far):
@@ -118,9 +91,15 @@
 
 def embed_kernel(
     channels,
-    px_ref,
+    slot_ref,
+    arrived_ref,
+    tiles_ref,
     w_ref,
     out_ref,
+    ordered,
+    tile_buf,
+    stage,
+    px,
     recv,
     w,
     lhs,
@@ -128,34 +107,55 @@
     got,
     total,
     local_sem,
+    tile_sem,
     send_sem,
     recv_sem,
     part_send,
     part_recv,
 ):
-    _, pairs, toks, _ = recv.shape
+    _, pairs, toks, _ = px.shape
     tiles, _, tile = total.shape
+    chunk_blocks = tile_buf.shape[1]
+    chunk = chunk_blocks // 2
+    steps = toks // chunk
     me = lax.axis_index("tensor")
-    load = pltpu.make_async_copy(w_ref, w.at[pl.ds(0, channels)], local_sem.at[0])
-    load.start()
-    own = pltpu.make_async_copy(px_ref.at[me], recv.at[0], local_sem.at[1])
-    own.start()
-    if channels < 2 * pairs:
-        w[channels:] = jnp.zeros((2 * pairs - channels,) + w.shape[1:], w.dtype)
-    greet([("tensor", far) for far in (1, 2, 3)])
-    moves = [
-        push(
-            px_ref.at[peer_of("tensor", far)],
-            recv.at[far],
-            send_sem.at[far - 1],
-            recv_sem.at[far - 1],
+
+    def fetch(step):
+        blocks = pl.ds(step * chunk_blocks, chunk_blocks)
+        slot = lax.rem(step, 2)
+        return pltpu.make_async_copy(tiles_ref.at[blocks], tile_buf.at[slot], tile_sem.at[slot])
+
+    def move(far, step):
+        rows = pl.ds(pl.multiple_of(step * chunk, chunk), chunk)
+        return push(
+            px.at[peer_of("tensor", far), :, rows],
+            recv.at[far - 1, :, rows],
+            send_sem.at[far - 1, step],
+            recv_sem.at[far - 1, step],
             "tensor",
             far,
         )
-        for far in (1, 2, 3)
-    ]
-    moves[2].start()
-    moves[0].start()
+
+    fetch(jnp.int32(0)).start()
+    if channels < 2 * pairs:
+        w[channels:] = jnp.zeros((2 * pairs - channels,) + w.shape[1:], w.dtype)
+    order_channels(arrived_ref, ordered)
+    greet([("tensor", far) for far in (1, 2, 3)])
+
+    @pl.loop(0, steps)
+    def _(step):
+        @pl.when(step + 1 < steps)
+        def _():
+            fetch(step + 1).start()
+
+        fetch(step).wait()
+        rows = pl.ds(pl.multiple_of(step * chunk, chunk), chunk)
+        px[:, :, rows] = regrid(step, slot_ref, ordered, tile_buf.at[lax.rem(step, 2)], stage)
+        move(3, step).start()
+        move(1, step).start()
+
+    load = pltpu.make_async_copy(w_ref, w.at[pl.ds(0, channels)], local_sem)
+    load.start()
 
     def back(far, i):
         return push(
@@ -170,7 +170,8 @@
     def multiply(far):
         @pl.loop(0, pairs)
         def _(j):
-            lhs[:, pl.ds(pl.multiple_of(j * LANES, LANES), LANES)] = recv[far, j]
+            block = px[me, j] if far == 0 else recv[far - 1, j]
+            lhs[:, pl.ds(pl.multiple_of(j * LANES, LANES), LANES)] = block
 
         @pl.loop(0, tiles)
         def _(i):
@@ -186,17 +187,26 @@
                 part[far - 1, i] = summed.astype(part.dtype)
                 back(far, i).start()
 
-    own.wait()
     load.wait()
     multiply(0)
-    moves[2].wait_send()
-    moves[1].start()
-    moves[2].wait_recv()
-    multiply(3)
-    moves[0].wait()
-    multiply(1)
-    moves[1].wait()
-    multiply(2)
+
+    @pl.loop(0, steps)
+    def _(step):
+        move(3, step).wait_send()
+        move(2, step).start()
+
+    for far in (3, 1, 2):
+
+        @pl.loop(0, steps)
+        def _(step):
+            move(far, step).wait_recv()
+
+        multiply(far)
+
+    @pl.loop(0, steps)
+    def _(step):
+        move(1, step).wait_send()
+        move(2, step).wait_send()
 
     @pl.loop(0, tiles)
     def _(i):
@@ -209,33 +219,47 @@
         out_ref[:, cols] = summed.astype(out_ref.dtype)
 
 
-def embed(pixels, weight, tile=512):
-    senders, pairs, toks, _ = pixels.shape
+def embed(slots, arrived, intersection_tiles, weight, chunk=16, tile=512):
     channels, sub_pix, width = weight.shape
+    n_slots, _, cells = arrived.shape
+    toks = intersection_tiles.shape[0] // 2
+    pairs = (channels + 1) // 2
+    half = round_up(pairs + 1, 8)
     tiles = width // tile
+    steps = toks // chunk
     return pl.pallas_call(
         functools.partial(embed_kernel, channels),
         out_shape=jax.ShapeDtypeStruct((toks, width), jnp.bfloat16),
-        in_specs=[pl.BlockSpec(memory_space=pl.ANY)] * 2,
+        in_specs=[
+            pl.BlockSpec(memory_space=pltpu.SMEM),
+            pl.BlockSpec(memory_space=pltpu.VMEM),
+            pl.BlockSpec(memory_space=pl.ANY),
+            pl.BlockSpec(memory_space=pl.ANY),
+        ],
         out_specs=pl.BlockSpec(memory_space=pltpu.VMEM),
         scratch_shapes=[
-            pltpu.VMEM(pixels.shape, jnp.bfloat16),
+            pltpu.VMEM((n_slots, 2 * half, cells), jnp.bfloat16),
+            pltpu.VMEM((2, 2 * chunk) + intersection_tiles.shape[1:], jnp.bfloat16),
+            pltpu.VMEM((4 * pairs * chunk, LANES), jnp.float32),
+            pltpu.VMEM((4, pairs, toks, LANES), jnp.bfloat16),
+            pltpu.VMEM((3, pairs, toks, LANES), jnp.bfloat16),
             pltpu.VMEM((2 * pairs, sub_pix, width), jnp.bfloat16),
             pltpu.VMEM((toks, pairs * LANES), jnp.bfloat16),
             pltpu.VMEM((3, tiles, toks, tile), jnp.bfloat16),
             pltpu.VMEM((3, tiles, toks, tile), jnp.bfloat16),
             pltpu.VMEM((tiles, toks, tile), jnp.float32),
+            pltpu.SemaphoreType.DMA,
             pltpu.SemaphoreType.DMA((2,)),
-            pltpu.SemaphoreType.DMA((3,)),
-            pltpu.SemaphoreType.DMA((3,)),
+            pltpu.SemaphoreType.DMA((3, steps)),
+            pltpu.SemaphoreType.DMA((3, steps)),
             pltpu.SemaphoreType.DMA((3, tiles)),
             pltpu.SemaphoreType.DMA((3, tiles)),
         ],
         compiler_params=pltpu.CompilerParams(
-            collective_id=0, has_side_effects=True, vmem_limit_bytes=50 * MIB
+            collective_id=0, has_side_effects=True, vmem_limit_bytes=54 * MIB
         ),
         name="embed",
-    )(pixels, weight)
+    )(slots, arrived, intersection_tiles, weight)
 
 
 def project_kernel(
@@ -522,8 +546,7 @@
         and lax.axis_size("patch") == 4
         and intersection_tiles.shape[0] % 32 == 0
     ):
-        pixels = regrid(arrived, intersection_tiles, intersection.reshape(-1))
-        own_rows = embed(pixels, emb_weight)
+        own_rows = embed(intersection.reshape(-1), arrived, intersection_tiles, emb_weight)
         query, keys, values = project_all(
             own_rows, norm_gain[None, :], jnp.transpose(attention_in, (1, 0, 2))
         )

time: 263 us -> 253 us (0.962)
  Pallas kernels: 230 us -> 220 us
    pallas_call x1 -> x0, Pallas kernels: 17.5 us -> none  [regrid(): pl.pallas_call(functools.partial(regrid_kernel, channels, toks), out_shap...]
    pallas_call x1, Pallas kernels: 126 us -> 133 us  [embed(): pl.pallas_call(functools.partial(embed_kernel, channels), out_shape=jax.S...]
where the time goes in v4:
time: 253 us; the launch traced here: 252 us
  Pallas kernels  220 us (87%)
  waiting for transfers between devices  15.7 us (6%)
  local copies, waits for them, and re-layouts  8.96 us (4%)
  starting transfers between devices  7.36 us (3%)
    pallas_call x1, Pallas kernels, embed(): pl.pallas_call(functools.partial(embed_kernel, channels), out_shape=jax.S...  133 us
    pallas_call x1, Pallas kernels, project_all(): pl.pallas_call(project_kernel, out_shape=(jax.ShapeDtypeStruct((4 * toks,...  47.7 us
    pallas_call x1, Pallas kernels, mix(): pl.pallas_call(mix_kernel, out_shape=jax.ShapeDtypeStruct(x.shape, jnp.bf...  39.6 us
    all_to_all x1, waiting for transfers between devices, on_device(): lax.all_to_all(payload, ('patch', 'tensor'), split_axis=0, concat_axis=0,...  15.7 us
    all_to_all x1, starting transfers between devices, on_device(): lax.all_to_all(payload, ('patch', 'tensor'), split_axis=0, concat_axis=0,...  7.36 us
  transfers between devices with their start and end apart: 1, of which 1 were waited for; matrix products, arithmetic and copies ran while one was open for 0% of the time, Pallas kernels for 0%

profile of v4, /device:TPU:0, one launch (start us, length us, event | category | flops | bytes accessed | tf_op | source)
XLA Modules:
  0.0 252.0 jit_solution(7853111874338943537)
XLA Ops:
  0.0 0.0 copy-start.3
  0.0 0.8 copy.15
  0.8 0.1 reshape.24
  0.9 3.3 %gather_fusion = bf16[32,69,128]{2,0,1:T(8,128)(2,1)S(1)} fusion(bf16[256,69,128]{2,0,1:T(8,128)(2,1)} %param.8, s32[1024]{0:T(1024)S(1)} %pad_clamp_fusion), kind=kCustom, calls=%fused_computation | custom fusion | bytes 1130624 | tf_op jit(solution)/shard_map/jit(_take)/gather | solution.py:538
  4.2 1.2 copy.16
  5.4 7.4 %all-to-all-start = ((bf16[16,2,69,128]{3,1,2,0:T(2,128)(2,1)}), bf16[16,2,69,128]{3,1,2,0:T(2,128)(2,1)S(1)}, u32[]{:S(2)}, u32[]{:S(2)}) async-start(bf16[16,2,69,128]{3,1,2,0:T(2,128)(2,1)} %copy.16), calls=%async_computation | async-start | bytes 1130496 | tf_op jit(solution)/shard_map/all_to_all | solution.py:541
  12.8 0.0 copy-done.3
  12.8 0.1 copy.14
  12.9 0.7 reshape.17.slot_ref
  13.6 15.7 %all-to-all-done = bf16[16,2,69,128]{3,1,2,0:T(2,128)(2,1)S(1)} async-done(((bf16[16,2,69,128]{3,1,2,0:T(2,128)(2,1)}), bf16[16,2,69,128]{3,1,2,0:T(2,128)(2,1)S(1)}, u32[]{:S(2)}, u32[]{:S(2)}) %all-to-all-start) | async-done | bytes 565280 | tf_op jit(solution)/shard_map/all_to_all | solution.py:541
  29.3 0.0 slice-start
  29.3 0.9 copy.17
  30.2 0.0 slice-start.1
  30.2 0.0 copy-start.2
  30.2 0.0 copy-start.1
  30.2 132.6 %embed.1.x_ref = bf16[128,2048]{1,0:T(8,128)(2,1)} custom-call(s32[512]{0:T(512)} %reshape.17.slot_ref, bf16[32,69,128]{2,1,0:T(8,128)(2,1)} %bitcast.13, bf16[256,2,128,128]{3,2,1,0:T(8,128)(2,1)} %tiles_ref.1, bf16[69,64,2048]{2,1,0:T(8,128)(2,1)} %w_ref.2), custom_call_target="tpu_custom_call" | custom-call | tf_op jit(solution)/shard_map/embed/pallas_call | solution.py:230
  162.8 0.0 slice-done
  162.8 0.0 slice-done.1
  162.8 0.0 copy-done.2
  162.8 0.0 copy-start
  162.8 1.0 copy-done
  163.9 47.7 %project_all.1 = (bf16[512,512]{1,0:T(8,128)(2,1)S(1)}, bf16[4,4,128,512]{3,2,1,0:T(8,128)(2,1)S(1)}, bf16[4,4,128,512]{3,2,1,0:T(8,128)(2,1)S(1)}) custom-call(bf16[128,2048]{1,0:T(8,128)(2,1)S(1)} %copy-done, f32[1,2048]{1,0:T(1,128)S(1)} %bitcast.11, bf16[3,2048,512]{2,1,0:T(8,128)(2,1)S(1)} %bitcast.8), custom_call_target="tpu_custom_call" | custom-call | tf_op jit(solution)/shard_map/project_all/pallas_call | solution.py:358
  211.6 0.0 copy-done.1
  211.6 39.6 %mix.1 = bf16[128,2048]{1,0:T(8,128)(2,1)S(1)} custom-call(bf16[512,512]{1,0:T(8,128)(2,1)S(1)} %get-tuple-element.8.q_ref, bf16[2048,512]{1,0:T(8,128)(2,1)S(1)} %bitcast.9, bf16[2048,512]{1,0:T(8,128)(2,1)S(1)} %bitcast.10, bf16[512,2048]{1,0:T(8,128)(2,1)S(1)} %copy-done.1, bf16[128,2048]{1,0:T(8,128)(2,1)S(1)} %copy-done), custom_call_target="tpu_custom_call" | custom-call | tf_op jit(solution)/shard_map/mix/pallas_call | solution.py:452
  251.2 0.8 copy.19
  (2 shorter events, 0.0 us)
Async XLA Ops:
  0.0 12.8 %copy-start.3 = (s32[256,2]{0,1:T(2,128)S(1)}, s32[256,2]{0,1:T(2,128)}, u32[]{:S(2)}) copy-start(s32[256,2]{0,1:T(2,128)} %param.11) | copy-start | bytes 6148
  5.4 23.9 %all-to-all-start = ((bf16[16,2,69,128]{3,1,2,0:T(2,128)(2,1)}), bf16[16,2,69,128]{3,1,2,0:T(2,128)(2,1)S(1)}, u32[]{:S(2)}, u32[]{:S(2)}) async-start(bf16[16,2,69,128]{3,1,2,0:T(2,128)(2,1)} %copy.16), calls=%async_computation | async-start | bytes 1130496 | tf_op jit(solution)/shard_map/all_to_all | solution.py:541
  29.3 133.5 %slice-start = ((s8[6291456]{0:T(1024)(128)(4,1)}), s8[4194304]{0:T(1024)(128)(4,1)S(1)}, s32[]{:S(2)}) async-start(s8[6291456]{0:T(1024)(128)(4,1)} %bitcast.6), calls=%async_computation.1 | async-start | bytes 8388608
  30.2 132.6 %slice-start.1 = ((s8[6291456]{0:T(1024)(128)(4,1)}), s8[2097152]{0:T(1024)(128)(4,1)S(1)}, s32[]{:S(2)}) async-start(s8[6291456]{0:T(1024)(128)(4,1)} %bitcast.6), calls=%async_computation.2 | async-start | bytes 4194304
  30.2 132.6 %copy-start.2 = (f32[2048]{0:T(1024)S(1)}, f32[2048]{0:T(1024)}, u32[]{:S(2)}) copy-start(f32[2048]{0:T(1024)} %param.13) | copy-start | bytes 24580
  30.2 181.3 %copy-start.1 = (bf16[512,2048]{1,0:T(8,128)(2,1)S(1)}, bf16[512,2048]{1,0:T(8,128)(2,1)}, u32[]{:S(2)}) copy-start(bf16[512,2048]{1,0:T(8,128)(2,1)} %w_ref.3) | copy-start | bytes 6291460
  162.8 1.0 copy-start
